TPU v7x, 128 devices: a whole 4x4x4 slice. The times are simulated.
128 devices in a mesh: dp: 32 (over x, z, y_lo), seq: 4 (over y_hi, core).
Axes of the slice: x: 4, y: 4 (y_hi: 2, y_lo: 2; y = y_hi * 2 + y_lo), z: 4, core: 2. Of those that a mesh axis runs over, the one named last changes fastest.
Arguments:
- tokens: bfloat16 [32, 1024, 1024], P('dp', 'seq'), may hold values from -6 to 6
- memory: bfloat16 [32, 1024, 1024], P('dp', 'seq'), may hold values from -6 to 6
- cotangent: bfloat16 [32, 1024, 1024], P('dp', 'seq'), may hold values from -12 to 12
- mem_len: int32 [32], P('dp'), may hold values from 0 to 1024, as said below
- value_route: int32 [32, 2, 1024, 4, 2], P('dp', None, 'seq'), may hold values from 0 to 4, all different within a row
- output_route: int32 [32, 1024, 4, 2], P('dp', 'seq'), may hold values from 0 to 4, all different within a row
- attn_norm_gain: bfloat16 [1024], replicated, may hold values from 0.5 to 1.5
- attn_norm_bias: bfloat16 [1024], replicated, may hold values from -1.25 to 1.25
- query_weight: bfloat16 [1024, 448], replicated, may hold values from -0.1875 to 0.1875
- key_weight: bfloat16 [1024, 448], replicated, may hold values from -0.1875 to 0.1875
- rel_weight: bfloat16 [1024, 448], replicated, may hold values from -0.1875 to 0.1875
- bias_u: bfloat16 [448], replicated, may hold values from -3 to 3
- bias_v: bfloat16 [448], replicated, may hold values from -3 to 3
- value_router: bfloat16 [1024, 20], replicated, may hold values from -0.09375 to 0.09375
- value_weight: bfloat16 [1024, 2240], replicated, may hold values from -0.1875 to 0.1875
- out_router: bfloat16 [1024, 20], replicated, may hold values from -0.09375 to 0.09375
- out_weight: bfloat16 [2240, 1024], replicated, may hold values from -3 to 3
- ffn_norm_gain: bfloat16 [1024], replicated, may hold values from 0.5 to 1.5
- ffn_norm_bias: bfloat16 [1024], replicated, may hold values from -1.25 to 1.25
- up_weight: bfloat16 [1024, 4096], replicated, may hold values from -0.1875 to 0.1875
- up_bias: bfloat16 [4096], replicated, may hold values from -1.25 to 1.25
- down_weight: bfloat16 [4096, 1024], replicated, may hold values from -0.09375 to 0.09375
- down_bias: bfloat16 [1024], replicated, may hold values from -1.25 to 1.25
Outputs:
- result: bfloat16 [32, 1024, 1024], P('dp', 'seq')
- grad_tokens: float32 [32, 1024, 1024], P('dp', 'seq')
- grad_attn_norm_gain: float32 [1024], P(('dp', 'seq'))
- grad_attn_norm_bias: float32 [1024], P(('dp', 'seq'))
- grad_query_weight: float32 [1024, 448], P(('dp', 'seq'))
- grad_key_weight: float32 [1024, 448], P(('dp', 'seq'))
- grad_rel_weight: float32 [1024, 448], P(('dp', 'seq'))
- grad_bias_u: float32 [448], replicated
- grad_bias_v: float32 [448], replicated
- grad_value_router: float32 [1024, 20], P(('dp', 'seq'))
- grad_value_weight: float32 [1024, 2240], P(('dp', 'seq'))
- grad_out_router: float32 [1024, 20], P(('dp', 'seq'))
- grad_out_weight: float32 [2240, 1024], P(None, ('dp', 'seq'))
- grad_ffn_norm_gain: float32 [1024], P(('dp', 'seq'))
- grad_ffn_norm_bias: float32 [1024], P(('dp', 'seq'))
- grad_up_weight: float32 [1024, 4096], P(('dp', 'seq'))
- grad_up_bias: float32 [4096], P(('dp', 'seq'))
- grad_down_weight: float32 [4096, 1024], P(('dp', 'seq'))
- grad_down_bias: float32 [1024], P(('dp', 'seq'))
- expert_counts: int32 [2, 4, 5], replicated
Inputs may be any that keep to these rules, and one draw needn't show every extreme that they name: `mem_len`: some item sees no memory row and some item sees all 1024. `value_route`: 2 different experts for each row and head. `output_route`: 2 different experts for each token and head.
All inputs are finite; a program needn't handle non-finite values.
Results may differ from a plain program's by a relative error of at most 0.02.
Values may be sent and summed in bfloat16 or wider, within the bound.
A program may use at most 384 MiB of HBM per device.

v0:
```python
from functools import partial
import math

import jax
import jax.numpy as jnp
from jax import lax
from jax.sharding import PartitionSpec as P

D = 1024
H = 4
DH = 112
E = 5
LEN = 1024


eps = 1e-05
masked_fill = -1e30


def layer_norm(values, norm_gain, norm_shift):
    center = values - jnp.mean(values, axis=-1, keepdims=True)
    spread = jnp.mean(center * center, axis=-1, keepdims=True)
    return center * lax.rsqrt(spread + eps) * norm_gain + norm_shift


def sinus_table(first_row, row_count, feat_count):
    places = (first_row + jnp.arange(row_count, dtype=jnp.int32)).astype(jnp.float32)
    frequency = jnp.exp(
        jnp.arange(feat_count // 2, dtype=jnp.int32).astype(jnp.float32)
        * (-2.0 * math.log(10000.0) / feat_count)
    )
    angles = places[:, None] * frequency[None, :]
    return jnp.concatenate([jnp.sin(angles), jnp.cos(angles)], axis=1)


def skew_rows(scores_far, key_span):
    lead_dims = scores_far.shape[:-2]
    row_block, window_len = (scores_far.shape[-2], scores_far.shape[-1])
    flattened = scores_far.reshape(lead_dims + (row_block * window_len,))
    trimmed = lax.slice_in_dim(
        flattened,
        row_block - 1,
        row_block - 1 + row_block * (window_len - 1),
        axis=flattened.ndim - 1,
    )
    return trimmed.reshape(lead_dims + (row_block, window_len - 1))[..., :key_span]


def product(spec, left, right):
    return jnp.einsum(spec, left, right, preferred_element_type=jnp.float32)


def body(
    tokens,
    memory,
    cotangent,
    mem_len,
    value_route,
    output_route,
    attn_norm_gain,
    attn_norm_bias,
    query_weight,
    key_weight,
    rel_weight,
    bias_u,
    bias_v,
    value_router,
    value_weight,
    out_router,
    out_weight,
    ffn_norm_gain,
    ffn_norm_bias,
    up_weight,
    up_bias,
    down_weight,
    down_bias,
):
    item_count, tok_rows = (tokens.shape[0], tokens.shape[1])
    key_span = 2 * LEN
    head_width = H * DH
    score_scale = DH ** (-0.5)
    seq_index = lax.axis_index("seq")
    first_query = seq_index * tok_rows
    both_rows = jnp.stack([memory, tokens], axis=1).astype(jnp.float32)
    normed_full, norm_back = jax.vjp(
        layer_norm,
        both_rows,
        attn_norm_gain.astype(jnp.float32),
        attn_norm_bias.astype(jnp.float32),
    )
    normed = normed_full.astype(jnp.bfloat16)
    tok_normed = normed[:, 1]
    query = product("nrd,dk->nrk", tok_normed, query_weight)
    query_u = (
        (query + bias_u.astype(jnp.float32))
        .astype(jnp.bfloat16)
        .reshape(item_count, tok_rows, H, DH)
    )
    query_v = (
        (query + bias_v.astype(jnp.float32))
        .astype(jnp.bfloat16)
        .reshape(item_count, tok_rows, H, DH)
    )
    key_own = product("nsrd,dk->nsrk", normed, key_weight).astype(jnp.bfloat16)
    picks = jnp.arange(E, dtype=jnp.int32)
    value_pick = jnp.sum((value_route[..., None] == picks).astype(jnp.float32), axis=4)
    value_logit = product("nsrd,dk->nsrk", normed, value_router).reshape(
        item_count, 2, tok_rows, H, E
    )
    value_sig = jax.nn.sigmoid(value_logit)
    value_gate = value_sig * value_pick
    value_experts = product("nsrd,dk->nsrk", normed, value_weight).reshape(
        item_count, 2, tok_rows, H, E, DH
    )
    value_own = (
        jnp.sum(value_gate[..., None] * value_experts, axis=4)
        .reshape(item_count, 2, tok_rows, head_width)
        .astype(jnp.bfloat16)
    )
    keys_all, values_all = (
        lax.all_gather(key_own, "seq", axis=2, tiled=True),
        lax.all_gather(value_own, "seq", axis=2, tiled=True),
    )
    keys_all = keys_all.reshape(item_count, key_span, H, DH)
    values_all = values_all.reshape(item_count, key_span, H, DH)
    sinus = sinus_table(0, key_span, D).astype(jnp.bfloat16)
    relative = product("td,dk->tk", sinus, rel_weight).astype(jnp.bfloat16)
    window_len = key_span + tok_rows - 1
    rel_rev = jnp.concatenate(
        [jnp.flip(relative, 0), jnp.zeros((LEN - 1, head_width), jnp.bfloat16)], axis=0
    )
    window_start = LEN - tok_rows - first_query
    rel_window = lax.dynamic_slice_in_dim(rel_rev, window_start, window_len, 0).reshape(
        window_len, H, DH
    )
    query_at = first_query + jnp.arange(tok_rows, dtype=jnp.int32)
    key_at = jnp.arange(key_span, dtype=jnp.int32)
    visible = (key_at[None, None, None, :] <= LEN + query_at[None, None, :, None]) & (
        key_at[None, None, None, :] >= LEN - mem_len[:, None, None, None]
    )

    def score_block():
        content = product("nihd,njhd->nhij", query_u, keys_all)
        far_scores = product("nihd,thd->nhit", query_v, rel_window)
        return jnp.where(
            visible, (content + skew_rows(far_scores, key_span)) * score_scale, masked_fill
        )

    scores = score_block()
    highest = jnp.max(scores, axis=-1, keepdims=True)
    weights = jnp.exp(scores - highest)
    total = jnp.sum(weights, axis=-1, keepdims=True)
    probs_low = (weights / total).astype(jnp.bfloat16)
    log_total = highest + jnp.log(total)
    attended = product("nhij,njhd->nihd", probs_low, values_all)
    out_pick = jnp.sum((output_route[..., None] == picks).astype(jnp.float32), axis=3)
    out_logit = product("nrd,dk->nrk", tok_normed, out_router).reshape(item_count, tok_rows, H, E)
    out_sig = jax.nn.sigmoid(out_logit)
    out_gate = out_sig * out_pick
    mixed = (
        (out_gate[..., None] * attended[:, :, :, None, :])
        .reshape(item_count, tok_rows, H * E * DH)
        .astype(jnp.bfloat16)
    )
    attn_out = product("nrk,kd->nrd", mixed, out_weight)
    resid = tokens.astype(jnp.float32) + attn_out
    normed_two_full, norm_two_back = jax.vjp(
        layer_norm, resid, ffn_norm_gain.astype(jnp.float32), ffn_norm_bias.astype(jnp.float32)
    )
    normed_two = normed_two_full.astype(jnp.bfloat16)
    before = product("nrd,df->nrf", normed_two, up_weight) + up_bias.astype(jnp.float32)
    hidden_full, gelu_back = jax.vjp(partial(jax.nn.gelu, approximate=False), before)
    hidden = hidden_full.astype(jnp.bfloat16)
    final = resid + product("nrf,fd->nrd", hidden, down_weight) + down_bias.astype(jnp.float32)
    result = final.astype(jnp.bfloat16)
    cot_full = cotangent.astype(jnp.float32)
    grad_down = product("nrf,nrd->fd", hidden, cotangent)
    grad_down_bias = jnp.sum(cot_full, axis=(0, 1))
    grad_hidden = product("nrd,fd->nrf", cotangent, down_weight)
    grad_before = gelu_back(grad_hidden)[0].astype(jnp.bfloat16)
    grad_up = product("nrd,nrf->df", normed_two, grad_before)
    grad_up_bias = jnp.sum(grad_before.astype(jnp.float32), axis=(0, 1))
    grad_normed_two = product("nrf,df->nrd", grad_before, up_weight)
    grad_resid_norm, grad_ffn_gain, grad_ffn_bias = norm_two_back(grad_normed_two)
    grad_resid = cot_full + grad_resid_norm
    grad_attn = grad_resid.astype(jnp.bfloat16)
    grad_out_weight = product("nrk,nrd->kd", mixed, grad_attn)
    grad_mixed = product("nrd,kd->nrk", grad_attn, out_weight).reshape(
        item_count, tok_rows, H, E, DH
    )
    grad_out_gate = jnp.sum(grad_mixed * attended[:, :, :, None, :], axis=-1)
    grad_attended = jnp.sum(grad_mixed * out_gate[..., None], axis=3).astype(jnp.bfloat16)
    grad_out_logit = (
        (grad_out_gate * out_pick * out_sig * (1.0 - out_sig))
        .reshape(item_count, tok_rows, H * E)
        .astype(jnp.bfloat16)
    )
    grad_out_router = product("nrd,nrk->dk", tok_normed, grad_out_logit)
    probs = jnp.exp(score_block() - log_total)
    grad_probs = product("nihd,njhd->nhij", grad_attended, values_all)
    inner_sum = jnp.sum(probs * grad_probs, axis=-1, keepdims=True)
    grad_raw = probs * (grad_probs - inner_sum) * score_scale
    grad_raw_low = grad_raw.astype(jnp.bfloat16)
    grad_query_u = product("nhij,njhd->nihd", grad_raw_low, keys_all)
    grad_keys = product("nhij,nihd->njhd", grad_raw_low, query_u)
    grad_values = product("nhij,nihd->njhd", probs_low, grad_attended)
    _, skew_back = jax.vjp(
        lambda far_scores: skew_rows(far_scores, key_span),
        jnp.zeros((item_count, H, tok_rows, window_len), jnp.float32),
    )
    grad_far = skew_back(grad_raw)[0].astype(jnp.bfloat16)
    grad_query_v = product("nhit,thd->nihd", grad_far, rel_window)
    grad_window = product("nhit,nihd->nthd", grad_far, query_v).reshape(
        item_count, window_len, head_width
    )
    grad_rev = lax.dynamic_update_slice_in_dim(
        jnp.zeros((item_count, key_span + LEN - 1, head_width), jnp.float32),
        grad_window,
        window_start,
        1,
    )
    grad_rel = jnp.flip(grad_rev[:, :key_span], 1)
    rel_share = lax.psum_scatter(
        grad_rel.astype(jnp.bfloat16), "seq", scatter_dimension=1, tiled=True
    )
    share_rows = rel_share.shape[1]
    sinus_share = sinus_table(seq_index * share_rows, share_rows, D).astype(jnp.bfloat16)
    grad_rel_weight = product("td,ntk->dk", sinus_share, rel_share)
    grad_bias_u = jnp.sum(grad_query_u, axis=(0, 1)).reshape(head_width)
    grad_bias_v = jnp.sum(grad_query_v, axis=(0, 1)).reshape(head_width)
    grad_query_low = (
        (grad_query_u + grad_query_v).reshape(item_count, tok_rows, head_width).astype(jnp.bfloat16)
    )
    key_grad_own, value_grad_own = (
        lax.psum_scatter(
            grad_keys.reshape(item_count, 2, LEN, head_width).astype(jnp.bfloat16),
            "seq",
            scatter_dimension=2,
            tiled=True,
        ).astype(jnp.float32),
        lax.psum_scatter(
            grad_values.reshape(item_count, 2, LEN, head_width).astype(jnp.bfloat16),
            "seq",
            scatter_dimension=2,
            tiled=True,
        ).astype(jnp.float32),
    )
    key_grad_low = key_grad_own.astype(jnp.bfloat16)
    value_grad = (
        value_grad_own.astype(jnp.bfloat16)
        .astype(jnp.float32)
        .reshape(item_count, 2, tok_rows, H, 1, DH)
    )
    grad_value_gate = jnp.sum(value_grad * value_experts, axis=-1)
    grad_experts = (
        (value_gate[..., None] * value_grad)
        .reshape(item_count, 2, tok_rows, H * E * DH)
        .astype(jnp.bfloat16)
    )
    grad_value_logit = (
        (grad_value_gate * value_pick * value_sig * (1.0 - value_sig))
        .reshape(item_count, 2, tok_rows, H * E)
        .astype(jnp.bfloat16)
    )
    grad_value_weight = product("nsrd,nsrk->dk", normed, grad_experts)
    grad_key_weight = product("nsrd,nsrk->dk", normed, key_grad_low)
    grad_value_router = product("nsrd,nsrk->dk", normed, grad_value_logit)
    grad_query_weight = product("nrd,nrk->dk", tok_normed, grad_query_low)
    grad_normed = (
        product("nsrk,dk->nsrd", grad_experts, value_weight)
        + product("nsrk,dk->nsrd", key_grad_low, key_weight)
        + product("nsrk,dk->nsrd", grad_value_logit, value_router)
    )
    tok_extra = product("nrk,dk->nrd", grad_query_low, query_weight) + product(
        "nrk,dk->nrd", grad_out_logit, out_router
    )
    grad_normed = grad_normed.at[:, 1].add(tok_extra)
    grad_both, grad_attn_gain, grad_attn_bias = norm_back(grad_normed)
    grad_tokens = grad_resid + grad_both[:, 1]
    counts = jnp.stack([jnp.sum(value_pick, axis=(0, 1, 2)), jnp.sum(out_pick, axis=(0, 1))])
    sum_u, sum_v, count_sum = lax.psum((grad_bias_u, grad_bias_v, counts), ("dp", "seq"))
    summed = (
        lax.psum_scatter(grad_attn_gain, ("dp", "seq"), scatter_dimension=0, tiled=True),
        lax.psum_scatter(grad_attn_bias, ("dp", "seq"), scatter_dimension=0, tiled=True),
        lax.psum_scatter(grad_query_weight, ("dp", "seq"), scatter_dimension=0, tiled=True),
        lax.psum_scatter(grad_key_weight, ("dp", "seq"), scatter_dimension=0, tiled=True),
        lax.psum_scatter(grad_rel_weight, ("dp", "seq"), scatter_dimension=0, tiled=True),
        lax.psum_scatter(grad_value_router, ("dp", "seq"), scatter_dimension=0, tiled=True),
        lax.psum_scatter(grad_value_weight, ("dp", "seq"), scatter_dimension=0, tiled=True),
        lax.psum_scatter(grad_out_router, ("dp", "seq"), scatter_dimension=0, tiled=True),
        lax.psum_scatter(grad_out_weight, ("dp", "seq"), scatter_dimension=1, tiled=True),
        lax.psum_scatter(grad_ffn_gain, ("dp", "seq"), scatter_dimension=0, tiled=True),
        lax.psum_scatter(grad_ffn_bias, ("dp", "seq"), scatter_dimension=0, tiled=True),
        lax.psum_scatter(grad_up, ("dp", "seq"), scatter_dimension=0, tiled=True),
        lax.psum_scatter(grad_up_bias, ("dp", "seq"), scatter_dimension=0, tiled=True),
        lax.psum_scatter(grad_down, ("dp", "seq"), scatter_dimension=0, tiled=True),
        lax.psum_scatter(grad_down_bias, ("dp", "seq"), scatter_dimension=0, tiled=True),
    )
    return (
        result,
        grad_tokens,
        summed[0],
        summed[1],
        summed[2],
        summed[3],
        summed[4],
        sum_u,
        sum_v,
        summed[5],
        summed[6],
        summed[7],
        summed[8],
        summed[9],
        summed[10],
        summed[11],
        summed[12],
        summed[13],
        summed[14],
        count_sum.astype(jnp.int32),
    )


def solution(mesh):
    in_specs = (
        P("dp", "seq", None),
        P("dp", "seq", None),
        P("dp", "seq", None),
        P("dp"),
        P("dp", None, "seq", None, None),
        P("dp", "seq", None, None),
        P(),
        P(),
        P(),
        P(),
        P(),
        P(),
        P(),
        P(),
        P(),
        P(),
        P(),
        P(),
        P(),
        P(),
        P(),
        P(),
        P(),
    )
    out_specs = (
        P("dp", "seq", None),
        P("dp", "seq", None),
        P(("dp", "seq")),
        P(("dp", "seq")),
        P(("dp", "seq"), None),
        P(("dp", "seq"), None),
        P(("dp", "seq"), None),
        P(),
        P(),
        P(("dp", "seq"), None),
        P(("dp", "seq"), None),
        P(("dp", "seq"), None),
        P(None, ("dp", "seq")),
        P(("dp", "seq")),
        P(("dp", "seq")),
        P(("dp", "seq"), None),
        P(("dp", "seq")),
        P(("dp", "seq"), None),
        P(("dp", "seq")),
        P(),
    )
    return jax.shard_map(body, mesh=mesh, in_specs=in_specs, out_specs=out_specs, check_vma=False)
```

profile of v0, /device:TPU:3, one launch (start us, length us, event | category | flops | bytes accessed | tf_op | source)
XLA Modules:
  0.0 5392.7 jit_solution(11242376684538053446)
XLA Ops:
  31.2 15.8 fusion.10
  50.4 31.8 rev.8
  91.4 9.8 copy.86
  101.2 13.9 reshape.996
  115.1 11.7 reshape.967
  126.8 11.5 slice.51
  138.3 11.1 reshape.998
  149.4 17.3 reshape.968
  201.5 16.6 multiply_convert_fusion.1
  218.2 12.1 convert_reduce_fusion
  230.2 7.4 fusion.82
  248.8 84.7 %copy.104 = bf16[1,2,1024,448]{1,3,0,2:T(8,128)(2,1)} copy(bf16[1,2,1024,448]{2,1,3,0:T(2,128)(2,1)} %convert_element_type.362) | data formatting | bytes 3670016
  333.5 210.4 %reshape.994 = bf16[1024,896]{1,0:T(8,128)(2,1)} reshape(bf16[1024,1,448,2]{3,2,1,0:T(8,128)(2,1)} %bitcast.71) | data formatting | bytes 3670016
  556.5 11.0 reshape.1000
  567.5 6.5 reshape.977
  574.0 7.4 pad.12
  587.7 13.6 convert_element_type.372
  606.3 16.3 dynamic_update_slice.3
  624.3 22.7 rev.9
  668.5 63.4 %reshape.995 = bf16[256,1,448,2]{3,2,1,0:T(8,128)(2,1)} reshape(bf16[256,896]{1,0:T(8,128)(2,1)} %reduce-scatter.31.cloned.1.call-done) | data formatting | bytes 917504
  731.8 27.5 copy.105
  793.4 9.9 fusion.122
  804.3 9.8 fusion.90
  820.4 7.3 fusion.58
  837.5 68.0 %all-reduce.11 = (f32[1024]{0:T(1024)S(1)}, f32[1024]{0:T(1024)S(1)}, f32[448]{0:T(512)}, f32[448]{0:T(512)}, f32[1024]{0:T(1024)S(1)}, /*index=5*/f32[1024]{0:T...) all-reduce(f32[1024]{0:T(1024)S(1)} %get-tuple-element.32, ...), channel_id=5, replica_groups=mesh['dp'=32,'seq'=4] {'dp','seq'}, use_global_device_ids=true, to_apply=%region_20.21.clone | all-reduce | flops 10152 | bytes 81216
  914.2 558.4 %reduce-scatter.15.cloned.1.call-done = f32[8,448]{1,0:T(8,128)} async-done(((f32[1024,448]{1,0:T(8,128)}), f32[8,448]{1,0:T(8,128)}) %reduce-scatter.15.cloned.1.call-update) | async-done | bytes 14352 | tf_op jit(solution)/shard_map/reduce_scatter | solution.py:285
  1472.7 637.3 %reduce-scatter.21.cloned.1.call-done = f32[8,448]{1,0:T(8,128)} async-done(((f32[1024,448]{1,0:T(8,128)}), f32[8,448]{1,0:T(8,128)}) %reduce-scatter.21.cloned.1.call-update) | async-done | bytes 14352 | tf_op jit(solution)/shard_map/reduce_scatter | solution.py:287
  2110.0 637.7 %reduce-scatter.17.cloned.1.call-done = f32[8,448]{1,0:T(8,128)} async-done(((f32[1024,448]{1,0:T(8,128)}), f32[8,448]{1,0:T(8,128)}) %reduce-scatter.17.cloned.1.call-update) | async-done | bytes 14352 | tf_op jit(solution)/shard_map/reduce_scatter | solution.py:286
  2747.6 650.9 %reduce-scatter.25.cloned.1.call-done = f32[2240,8]{0,1:T(8,128)} async-done(((f32[2240,1024]{0,1:T(8,128)}), f32[2240,8]{0,1:T(8,128)}) %reduce-scatter.25.cloned.1.call-update) | async-done | bytes 71696 | tf_op jit(solution)/shard_map/reduce_scatter | solution.py:291
  3398.5 650.0 %reduce-scatter.23.cloned.1.call-done = f32[8,2240]{1,0:T(8,128)} async-done(((f32[1024,2240]{1,0:T(8,128)}), f32[8,2240]{1,0:T(8,128)}) %reduce-scatter.23.cloned.1.call-update) | async-done | bytes 71696 | tf_op jit(solution)/shard_map/reduce_scatter | solution.py:289
  4048.6 669.8 %reduce-scatter.27.cloned.1.call-done = f32[8,4096]{1,0:T(8,128)} async-done(((f32[1024,4096]{1,0:T(8,128)}), f32[8,4096]{1,0:T(8,128)}) %reduce-scatter.27.cloned.1.call-update) | async-done | bytes 131088 | tf_op jit(solution)/shard_map/reduce_scatter | solution.py:294
  4718.4 667.6 %reduce-scatter.29.cloned.1.call-done = f32[32,1024]{1,0:T(8,128)} async-done(((f32[4096,1024]{1,0:T(8,128)}), f32[32,1024]{1,0:T(8,128)}) %reduce-scatter.29.cloned.1.call-update) | async-done | bytes 131088 | tf_op jit(solution)/shard_map/reduce_scatter | solution.py:296
  (335 shorter events, 187.4 us)
Async XLA Ops:
  7.2 39.8 copy-start
  7.2 159.9 %all-gather.6.cloned.1.call-start = ((), (), s32[]{:S(2)}) async-start(), calls=%async_computation.20 | async-start | bytes 2293760 | tf_op jit(solution)/shard_map/all_gather | solution.py:121
  8.8 17.8 copy-start.53
  10.5 16.2 copy-start.58
  11.2 18.6 copy-start.51
  11.9 17.9 copy-start.67
  15.0 173.3 %all-gather.4.cloned.1.call-start = ((), (), s32[]{:S(2)}) async-start(), calls=%async_computation.10 | async-start | bytes 2293760 | tf_op jit(solution)/shard_map/all_gather | solution.py:122
  26.0 642.4 %reduce-scatter.31.cloned.1.call-start = ((), (), s32[]{:S(2)}) async-start(), calls=%async_computation.21 | async-start | bytes 2293760
  26.6 20.3 copy-start.63
  29.7 54.8 %copy-start.35 = (f32[256,4,5]{0,1,2:T(4,128)}, f32[256,4,5]{0,1,2:T(4,128)S(1)}, u32[]{:S(2)}) copy-start(f32[256,4,5]{0,1,2:T(4,128)S(1)} %get-tuple-element.42) | copy-start | bytes 61444
  31.2 54.6 %copy-start.17 = (bf16[1,1,256,1024]{3,2,1,0:T(8,128)(2,1)}, bf16[1,1,256,1024]{3,2,1,0:T(8,128)(2,1)S(1)}, u32[]{:S(2)}) copy-start(bf16[1,1,256,1024]{3,2,1,0:T(8,128)(2,1)S(1)} %fusion.76) | copy-start | bytes 1572868
  50.4 35.3 copy-start.32
  86.2 90.6 %copy-start.28 = (bf16[256,448]{0,1:T(8,128)(2,1)}, bf16[256,448]{0,1:T(8,128)(2,1)S(1)}, u32[]{:S(2)}) copy-start(bf16[256,448]{0,1:T(8,128)(2,1)S(1)} %get-tuple-element.65) | copy-start | bytes 688132
  91.3 146.3 %copy-start.39 = (f32[1024]{0:T(1024)}, f32[1024]{0:T(1024)S(1)}, u32[]{:S(2)}) copy-start(f32[1024]{0:T(1024)S(1)} %convert_element_type.348) | copy-start | bytes 12292
  91.4 110.1 %copy-start.41 = (f32[1024]{0:T(1024)}, f32[1024]{0:T(1024)S(1)}, u32[]{:S(2)}) copy-start(f32[1024]{0:T(1024)S(1)} %convert_element_type.349) | copy-start | bytes 12292
  201.2 36.5 copy-start.13
  201.2 36.5 copy-start.56
  201.5 36.2 copy-start.61
  201.5 16.7 copy-start.20
  543.9 226.8 %reduce-scatter.19.cloned.1.call-start = ((), (), s32[]{:S(2)}) async-start(), calls=%async_computation.14 | async-start | bytes 2293760 | tf_op jit(solution)/shard_map/reduce_scatter | solution.py:223
  587.7 13.6 copy-start.31
  622.6 24.5 copy-start.29
  647.1 126.9 %reduce-scatter.13.cloned.1.call-start = ((), (), s32[]{:S(2)}) async-start(), calls=%async_computation.11 | async-start | bytes 2293760 | tf_op jit(solution)/shard_map/reduce_scatter | solution.py:235
  657.8 255.1 %all-reduce.15.cloned.1.call-start = ((), (), s32[]{:S(2)}) async-start(), calls=%async_computation.22 | async-start | bytes 2097152
  764.2 708.5 %reduce-scatter.15.cloned.1.call-start = ((), (), s32[]{:S(2)}) async-start(), calls=%async_computation.12 | async-start | bytes 2113536 | tf_op jit(solution)/shard_map/reduce_scatter | solution.py:285
  766.1 1343.9 %reduce-scatter.21.cloned.1.call-start = ((), (), s32[]{:S(2)}) async-start(), calls=%async_computation.15 | async-start | bytes 2113536 | tf_op jit(solution)/shard_map/reduce_scatter | solution.py:287
  773.9 1973.8 %reduce-scatter.17.cloned.1.call-start = ((), (), s32[]{:S(2)}) async-start(), calls=%async_computation.13 | async-start | bytes 2113536 | tf_op jit(solution)/shard_map/reduce_scatter | solution.py:286
  777.4 2621.1 %reduce-scatter.25.cloned.1.call-start = ((), (), s32[]{:S(2)}) async-start(), calls=%async_computation.17 | async-start | bytes 9510912 | tf_op jit(solution)/shard_map/reduce_scatter | solution.py:291
  783.8 3264.7 %reduce-scatter.23.cloned.1.call-start = ((), (), s32[]{:S(2)}) async-start(), calls=%async_computation.16 | async-start | bytes 9510912 | tf_op jit(solution)/shard_map/reduce_scatter | solution.py:289
  792.2 3926.1 %reduce-scatter.27.cloned.1.call-start = ((), (), s32[]{:S(2)}) async-start(), calls=%async_computation.18 | async-start | bytes 16908288 | tf_op jit(solution)/shard_map/reduce_scatter | solution.py:294
  803.3 4582.7 %reduce-scatter.29.cloned.1.call-start = ((), (), s32[]{:S(2)}) async-start(), calls=%async_computation.19 | async-start | bytes 16908288 | tf_op jit(solution)/shard_map/reduce_scatter | solution.py:296
  835.3 4550.7 %copy-start.1 = (bf16[1024,448]{0,1:T(8,128)(2,1)S(1)}, bf16[1024,448]{0,1:T(8,128)(2,1)}, u32[]{:S(2)}) copy-start(bf16[1024,448]{0,1:T(8,128)(2,1)} %param.35) | copy-start | bytes 2752516
  (76 other events, 294.8 us)
Sparse Core Ops, SparseCore 0:
  15.1 28.1 all-gather.5
  45.6 24.8 all-gather.3
  544.0 39.1 reduce-scatter.30
  647.2 38.9 reduce-scatter.18
  688.6 36.1 reduce-scatter.12
  764.3 148.5 all-reduce.14
  915.9 556.7 reduce-scatter.14
  1475.7 634.2 reduce-scatter.20
  2112.9 634.7 reduce-scatter.16
  2750.6 647.9 reduce-scatter.24
  3401.6 646.8 reduce-scatter.22
  4051.5 666.8 reduce-scatter.26
  4721.4 664.4 reduce-scatter.28
where the time goes:
time: 5490 us; the launch traced here: 5390 us
  waiting for transfers between devices  4480 us (82%)
  local copies, waits for them, and re-layouts  632 us (12%)
  matrix products  152 us (3%)
  blocking collectives  68 us (1%)
    reduce_scatter x1, waiting for transfers between devices, body(): lax.psum_scatter(grad_up, ('dp', 'seq'), scatter_dimension=0, tiled=True)  670 us
    reduce_scatter x1, waiting for transfers between devices, body(): lax.psum_scatter(grad_down, ('dp', 'seq'), scatter_dimension=0, tiled=True)  668 us
    reduce_scatter x1, waiting for transfers between devices, body(): lax.psum_scatter(grad_out_weight, ('dp', 'seq'), scatter_dimension=1, til...  651 us
    reduce_scatter x1, waiting for transfers between devices, body(): lax.psum_scatter(grad_value_weight, ('dp', 'seq'), scatter_dimension=0, t...  650 us
    reduce_scatter x1, waiting for transfers between devices, body(): lax.psum_scatter(grad_key_weight, ('dp', 'seq'), scatter_dimension=0, til...  638 us
    reduce_scatter x1, waiting for transfers between devices, body(): lax.psum_scatter(grad_rel_weight, ('dp', 'seq'), scatter_dimension=0, til...  637 us
    reduce_scatter x1, waiting for transfers between devices, body(): lax.psum_scatter(grad_query_weight, ('dp', 'seq'), scatter_dimension=0, t...  558 us
    unnamed x206, local copies, waits for them, and re-layouts  446 us
  transfers between devices with their start and end apart: 13, of which 8 were waited for; matrix products, arithmetic and copies ran while one was open for 8% of the time, Pallas kernels for 0%

commit v1 on v0

v1 whole, which is shorter than its diff:
```python
from functools import partial
import math

import jax
import jax.numpy as jnp
from jax import lax
from jax.experimental import pallas as pl
from jax.experimental.pallas import tpu as pltpu
from jax.sharding import PartitionSpec as P

D = 1024
H = 4
DH = 112
E = 5
FF = 4096
LEN = 1024
SLOT = 128
BLOCK = 256
EXPERTS = 2 * E * SLOT
KEY_AT = EXPERTS
QUERY_AT = KEY_AT + 2 * SLOT
ROUTER_AT = QUERY_AT + 2 * SLOT
WIDE = ROUTER_AT + SLOT
SCALE = DH ** (-0.5)
MASKED = -1e30
EPS = 1e-05
BF16 = jnp.bfloat16
F32 = jnp.float32
VMEM_BYTES = 58 * 1024 * 1024
IN_VMEM = pl.BlockSpec(memory_space=pltpu.VMEM)
IN_SMEM = pl.BlockSpec(memory_space=pltpu.SMEM)
MESH = pl.DeviceIdType.MESH


def dot(left, right, left_dim=1, right_dim=0):
    return lax.dot_general(
        left, right, (((left_dim,), (right_dim,)), ((), ())), preferred_element_type=F32
    )


def struct(shape, kind=BF16):
    return jax.ShapeDtypeStruct(shape, kind)


def local_call(kernel, out_shape, scratch_shapes=(), smem=0, vmem=0, **kw):
    return pl.pallas_call(
        kernel,
        out_shape=out_shape,
        in_specs=[IN_SMEM] * smem + [IN_VMEM] * vmem,
        out_specs=[IN_VMEM] * len(out_shape),
        scratch_shapes=scratch_shapes,
        compiler_params=pltpu.CompilerParams(vmem_limit_bytes=VMEM_BYTES),
        **kw,
    )


def centered(rows):
    center = rows - jnp.mean(rows, axis=1, keepdims=True)
    inverse = lax.rsqrt(jnp.mean(center * center, axis=1, keepdims=True) + EPS)
    return center * inverse, inverse


def norm_back(grad, scaled, inverse, gain):
    through = grad * gain
    return inverse * (
        through
        - jnp.mean(through, axis=1, keepdims=True)
        - scaled * jnp.mean(through * scaled, axis=1, keepdims=True)
    )


def picked(route, head, expert):
    return (route[:, 2 * head : 2 * head + 1] == expert) | (
        route[:, 2 * head + 1 : 2 * head + 2] == expert
    )


def pick_of(route, core, pair, expert):
    one = picked(route, 2 * pair, expert)
    two = picked(route, 2 * pair + 1, expert)
    return jnp.where(core == 0, one.astype(F32), two.astype(F32))


def prepare_kernel(spot, value_weight, key_weight, query_weight, rel_weight, value_router, out_router, out_weight, wide, rel, out_wide):
    core = spot[0]
    blank = jnp.zeros((SLOT - DH, D), BF16)

    def fill(target, slot, source, start):
        target[slot : slot + DH, :] = source[pl.ds(pl.multiple_of(start, DH), DH), :]
        target[slot + DH : slot + SLOT, :] = blank

    for pair in range(2):
        head = 2 * pair + core
        for expert in range(E):
            slot = (pair * E + expert) * SLOT
            fill(wide, slot, value_weight, (head * E + expert) * DH)
            fill(out_wide, slot, out_weight, (head * E + expert) * DH)
        fill(wide, KEY_AT + pair * SLOT, key_weight, head * DH)
        fill(wide, QUERY_AT + pair * SLOT, query_weight, head * DH)
    fill(rel, 0, rel_weight, (2 * spot[1] + core) * DH)
    routers = []
    for router in (value_router, out_router):
        for pair in range(2):
            one = router[2 * pair * E : (2 * pair + 1) * E, :].astype(F32)
            two = router[(2 * pair + 1) * E : (2 * pair + 2) * E, :].astype(F32)
            routers.append(jnp.where(core == 0, one, two))
    routers.append(jnp.zeros((SLOT - 4 * E, D), F32))
    wide[ROUTER_AT:, :] = jnp.concatenate(routers, axis=0).astype(BF16)


def prepare(spot, value_weight, key_weight, query_weight, rel_weight, value_router, out_router, out_weight):
    return local_call(
        prepare_kernel, [struct((WIDE, D)), struct((SLOT, D)), struct((EXPERTS, D))], smem=1, vmem=7
    )(spot, value_weight.T, key_weight.T, query_weight.T, rel_weight.T, value_router.T, out_router.T, out_weight)


def project_kernel(spot, rows, gain, shift, wide, route, normed, experts, logits, pay, full):
    step = pl.program_id(0)
    scaled, _ = centered(rows[...].astype(F32))
    low = (scaled * gain[...].astype(F32) + shift[...].astype(F32)).astype(BF16)
    normed[...] = low
    full[...] = dot(low, wide[...], 1, 1)
    experts[...] = full[:, :EXPERTS].astype(BF16)
    logit = full[:, ROUTER_AT:WIDE]
    logits[...] = logit
    gate = jax.nn.sigmoid(logit)
    routes = route[...]
    for pair in range(2):
        total = jnp.zeros((BLOCK, SLOT), F32)
        for expert in range(E):
            slot = pair * E + expert
            weight = gate[:, slot : slot + 1] * pick_of(routes, spot[0], pair, expert)
            total += weight * full[:, slot * SLOT : (slot + 1) * SLOT]
        pay[pair, step] = full[:, KEY_AT + pair * SLOT : KEY_AT + (pair + 1) * SLOT].astype(BF16)
        pay[pair, 4 + step] = total.astype(BF16)

        def keep_query(pair=pair):
            pay[pair, 6 + step] = full[:, QUERY_AT + pair * SLOT : QUERY_AT + (pair + 1) * SLOT].astype(BF16)

        pl.when(step >= 2)(keep_query)


def project(spot, rows, gain, shift, wide, route):
    block = lambda width: pl.BlockSpec((BLOCK, width), lambda step: (step, 0))
    fixed = lambda *shape: pl.BlockSpec(shape, lambda step: (0,) * len(shape))
    return pl.pallas_call(
        project_kernel,
        grid=(4,),
        out_shape=[struct((4 * BLOCK, D)), struct((4 * BLOCK, EXPERTS)), struct((4 * BLOCK, SLOT), F32), struct((2, 10, BLOCK, SLOT))],
        in_specs=[IN_SMEM, block(D), fixed(1, D), fixed(1, D), fixed(WIDE, D), block(2 * H)],
        out_specs=[block(D), block(EXPERTS), block(SLOT), fixed(2, 10, BLOCK, SLOT)],
        scratch_shapes=[pltpu.VMEM((BLOCK, WIDE), F32)],
        compiler_params=pltpu.CompilerParams(vmem_limit_bytes=VMEM_BYTES),
    )(spot, rows, gain, shift, wide, route)


def spots_of(core, chip):
    return [
        chip * 512 + core * BLOCK,
        chip * 512 + (1 - core) * BLOCK,
        (1 - chip) * 512 + core * BLOCK,
        (1 - chip) * 512 + (1 - core) * BLOCK,
    ]


def rows_at(start):
    return pl.ds(pl.multiple_of(start, BLOCK), BLOCK)


def attention_kernel(spot, own, peer, bias_u, bias_v, far_rel, attended, probs, keys, values, qu, qv, back):
    shown = spot[2]
    places = spots_of(spot[0], spot[1])
    for chip, pay in ((0, own), (1, peer)):
        for side in range(2):
            start = places[2 * chip + side]
            keys[rows_at(start), :] = pay[side]
            keys[rows_at(start + LEN), :] = pay[2 + side]
            values[rows_at(start), :] = pay[4 + side]
            values[rows_at(start + LEN), :] = pay[6 + side]
            query = pay[8 + side].astype(F32)
            qu[rows_at(start), :] = (query + bias_u[...]).astype(BF16)
            qv[rows_at(start), :] = (query + bias_v[...]).astype(BF16)
    for block in range(LEN // BLOCK):
        rows = pl.ds(block * BLOCK, BLOCK)
        width = LEN + (block + 1) * BLOCK
        first_far = 2 * LEN - width
        content = dot(qu[rows, :], keys[:width, :], 1, 1)
        far = dot(qv[rows, :], far_rel[first_far:, :], 1, 1)
        near = pltpu.roll(far, width - BLOCK + 1, 1, stride=1, stride_axis=0)
        row_at = lax.broadcasted_iota(jnp.int32, (BLOCK, width), 0) + (LEN + block * BLOCK)
        key_at = lax.broadcasted_iota(jnp.int32, (BLOCK, width), 1)
        visible = (key_at <= row_at) & (key_at >= LEN - shown)
        scores = jnp.where(visible, (content + near) * SCALE, MASKED)
        highest = jnp.max(scores, axis=1, keepdims=True)
        weights = jnp.exp(scores - highest)
        total = jnp.sum(weights, axis=1, keepdims=True)
        low = (weights * (1.0 / total)).astype(BF16)
        probs[rows, :width] = low
        attended[rows, :] = dot(low, values[:width, :], 1, 0)
    for number, start in enumerate(places):
        back[number] = attended[rows_at(start), :].astype(BF16)


def attention(spot, own, peer, bias_u, bias_v, far_rel):
    return local_call(
        attention_kernel,
        [
            struct((LEN, SLOT), F32),
            struct((LEN, 2 * LEN)),
            struct((2 * LEN, SLOT)),
            struct((2 * LEN, SLOT)),
            struct((LEN, SLOT)),
            struct((LEN, SLOT)),
            struct((4, BLOCK, SLOT)),
        ],
        smem=1,
        vmem=5,
    )(spot, own, peer, bias_u, bias_v, far_rel)


def two_heads(chip, own, peer):
    first = jnp.where(chip == 0, own.astype(F32), peer.astype(F32))
    second = jnp.where(chip == 0, peer.astype(F32), own.astype(F32))
    return first, second


def mix_kernel(spot, own, peer, logits, route, out_wide, mixed, partial_out):
    heads = two_heads(spot[1], own[...].reshape(2 * BLOCK, SLOT), peer[...].reshape(2 * BLOCK, SLOT))
    gate = jax.nn.sigmoid(logits[2 * BLOCK :, :])
    routes = route[...]
    for pair in range(2):
        for expert in range(E):
            slot = pair * E + expert
            weight = gate[:, 2 * E + slot : 2 * E + slot + 1] * pick_of(routes, spot[0], pair, expert)
            mixed[:, slot * SLOT : (slot + 1) * SLOT] = (weight * heads[pair]).astype(BF16)
    partial_out[...] = dot(mixed[...], out_wide[...]).astype(BF16)


def mix(spot, own, peer, logits, route, out_wide):
    return local_call(
        mix_kernel, [struct((2 * BLOCK, EXPERTS)), struct((2 * BLOCK, D))], smem=1, vmem=5
    )(spot, own, peer, logits, route, out_wide)


def feed_kernel(
    spot,
    rows,
    part_mine,
    part_theirs,
    cot,
    gain,
    shift,
    up,
    up_bias,
    down,
    down_bias,
    resid,
    final_mine,
    final_theirs,
    grad_part,
    grad_up,
    grad_up_bias,
    grad_down,
    low,
    low_turned,
    sum_out,
    sum_grad,
):
    step = pl.program_id(0)

    def first():
        for side in range(2):
            here = slice(side * BLOCK, (side + 1) * BLOCK)
            there = slice((1 - side) * BLOCK, (2 - side) * BLOCK)
            total = rows[here, :].astype(F32) + (part_mine[here, :].astype(F32) + part_theirs[there, :].astype(F32))
            resid[here, :] = total
            scaled, _ = centered(total)
            low[here, :] = (scaled * gain[...].astype(F32) + shift[...].astype(F32)).astype(BF16)
        low_turned[...] = low[...].T
        sum_out[...] = jnp.zeros_like(sum_out)
        sum_grad[...] = jnp.zeros_like(sum_grad)

    pl.when(step == 0)(first)
    before = dot(low[...], up[...]) + up_bias[...].astype(F32)
    below = 0.5 * (1.0 + lax.erf(before * (0.5**0.5)))
    hidden = (before * below).astype(BF16)
    slope = below + before * (jnp.exp(-0.5 * before * before) * ((2.0 * math.pi) ** -0.5))
    grad_before = dot(cot[...], down[...], 1, 1) * slope
    grad_low = grad_before.astype(BF16)
    grad_up_bias[...] = jnp.sum(grad_low.astype(F32), axis=0, keepdims=True)
    sum_out[...] += dot(hidden, down[...])
    sum_grad[...] += dot(grad_low, up[...], 1, 1)
    grad_up[...] = dot(low_turned[...], grad_low).astype(BF16)
    grad_down[...] = dot(hidden, cot[...], 0, 0).astype(BF16)

    def last():
        final_mine[...] = resid[:BLOCK, :] + sum_out[:BLOCK, :] + down_bias[...].astype(F32)
        final_theirs[...] = sum_out[BLOCK:, :].astype(BF16)
        grad_part[...] = sum_grad[...].astype(BF16)

    pl.when(step == pl.num_programs(0) - 1)(last)


def feed(spot, rows, part_mine, part_theirs, cot, gain, shift, up, up_bias, down, down_bias):
    fixed = lambda *shape: pl.BlockSpec(shape, lambda step, spot: (0,) * len(shape))
    steps = FF // 2 // BLOCK
    columns = lambda count: pl.BlockSpec((count, BLOCK), lambda step, spot: (0, spot[0] * steps + step))
    return pl.pallas_call(
        feed_kernel,
        grid_spec=pltpu.PrefetchScalarGridSpec(
            num_scalar_prefetch=1,
            grid=(steps,),
            in_specs=[
                pl.BlockSpec((2 * BLOCK, D), lambda step, spot: (1, 0)),
                fixed(2 * BLOCK, D),
                fixed(2 * BLOCK, D),
                fixed(2 * BLOCK, D),
                fixed(1, D),
                fixed(1, D),
                columns(D),
                columns(1),
                pl.BlockSpec((BLOCK, D), lambda step, spot: (spot[0] * steps + step, 0)),
                fixed(1, D),
            ],
            out_specs=[
                fixed(2 * BLOCK, D),
                fixed(BLOCK, D),
                fixed(BLOCK, D),
                fixed(2 * BLOCK, D),
                pl.BlockSpec((D, BLOCK), lambda step, spot: (0, step)),
                pl.BlockSpec((1, BLOCK), lambda step, spot: (0, step)),
                pl.BlockSpec((BLOCK, D), lambda step, spot: (step, 0)),
            ],
            scratch_shapes=[
                pltpu.VMEM((2 * BLOCK, D), BF16),
                pltpu.VMEM((D, 2 * BLOCK), BF16),
                pltpu.VMEM((2 * BLOCK, D), F32),
                pltpu.VMEM((2 * BLOCK, D), F32),
            ],
        ),
        out_shape=[
            struct((2 * BLOCK, D), F32),
            struct((BLOCK, D), F32),
            struct((BLOCK, D)),
            struct((2 * BLOCK, D)),
            struct((D, FF // 2)),
            struct((1, FF // 2), F32),
            struct((FF // 2, D)),
        ],
        compiler_params=pltpu.CompilerParams(vmem_limit_bytes=VMEM_BYTES),
    )(spot, rows, part_mine, part_theirs, cot, gain, shift, up, up_bias, down, down_bias)


def unmix_kernel(
    spot,
    resid,
    grad_mine,
    grad_theirs,
    cot,
    gain,
    own,
    peer,
    mixed,
    logits,
    route,
    out_wide,
    final_mine,
    final_theirs,
    grad_resid,
    pay,
    grad_logit,
    grad_out,
    sums,
    result,
    grad_low,
    grad_mixed,
):
    result[...] = (final_mine[...] + final_theirs[...].astype(F32)).astype(BF16)
    for side in range(2):
        here = slice(side * BLOCK, (side + 1) * BLOCK)
        there = slice((1 - side) * BLOCK, (2 - side) * BLOCK)
        scaled, inverse = centered(resid[here, :])
        grad = grad_mine[here, :].astype(F32) + grad_theirs[there, :].astype(F32)
        above = cot[here, :].astype(F32)
        total = above + norm_back(grad, scaled, inverse, gain[...].astype(F32))
        grad_low[here, :] = total.astype(BF16)
        if side == 0:
            grad_resid[...] = total
            sums[0:1, :] = jnp.sum(grad * scaled, axis=0, keepdims=True)
            sums[1:2, :] = jnp.sum(grad, axis=0, keepdims=True)
            sums[2:3, :] = jnp.sum(above, axis=0, keepdims=True)
    grad_mixed[...] = dot(grad_low[...], out_wide[...], 1, 1)
    heads = two_heads(spot[1], own[...].reshape(2 * BLOCK, SLOT), peer[...].reshape(2 * BLOCK, SLOT))
    gate = jax.nn.sigmoid(logits[2 * BLOCK :, :])
    routes = route[...]
    lane = lax.broadcasted_iota(jnp.int32, (2 * BLOCK, SLOT), 1)
    logit_sum = jnp.zeros((2 * BLOCK, SLOT), F32)
    totals = []
    for pair in range(2):
        total = jnp.zeros((2 * BLOCK, SLOT), F32)
        for expert in range(E):
            slot = pair * E + expert
            sig = gate[:, 2 * E + slot : 2 * E + slot + 1]
            pick = pick_of(routes, spot[0], pair, expert)
            part = grad_mixed[:, slot * SLOT : (slot + 1) * SLOT]
            total += part * (sig * pick)
            grad_gate = jnp.sum(part * heads[pair], axis=1, keepdims=True)
            logit_sum += jnp.where(lane == 2 * E + slot, grad_gate * pick * sig * (1.0 - sig), 0.0)
        totals.append(total)
    grad_logit[...] = logit_sum.astype(BF16)
    mine = jnp.where(spot[1] == 0, totals[0], totals[1]).astype(BF16)
    other = jnp.where(spot[1] == 0, totals[1], totals[0]).astype(BF16)
    pay[0, 0], pay[0, 1] = mine[:BLOCK], mine[BLOCK:]
    pay[1, 0], pay[1, 1] = other[:BLOCK], other[BLOCK:]
    grad_out[...] = dot(grad_low[...], mixed[...], 0, 0).astype(BF16)


def unmix(spot, resid, grad_mine, grad_theirs, cot, gain, own, peer, mixed, logits, route, out_wide, final_mine, final_theirs):
    return local_call(
        unmix_kernel,
        [
            struct((BLOCK, D), F32),
            struct((2, 2, BLOCK, SLOT)),
            struct((2 * BLOCK, SLOT)),
            struct((D, EXPERTS)),
            struct((8, D), F32),
            struct((BLOCK, D)),
        ],
        [pltpu.VMEM((2 * BLOCK, D), BF16), pltpu.VMEM((2 * BLOCK, EXPERTS), F32)],
        smem=1,
        vmem=13,
    )(spot, resid, grad_mine, grad_theirs, cot, gain, own, peer, mixed, logits, route, out_wide, final_mine, final_theirs)


def attention_back_kernel(
    spot,
    own,
    peer,
    qu,
    qv,
    keys,
    values,
    far_rel,
    probs,
    attended,
    pay,
    sums,
    grad_far,
    grad_out,
    grad_query,
    key_sum,
    value_sum,
    far_sum,
):
    places = spots_of(spot[0], spot[1])
    for chip, given in ((0, own), (1, peer)):
        for side in range(2):
            grad_out[rows_at(places[2 * chip + side]), :] = given[side]
    key_sum[...] = jnp.zeros_like(key_sum)
    value_sum[...] = jnp.zeros_like(value_sum)
    far_sum[...] = jnp.zeros_like(far_sum)
    sum_u = jnp.zeros((1, SLOT), F32)
    sum_v = jnp.zeros((1, SLOT), F32)
    down = lax.broadcasted_iota(jnp.int32, (BLOCK, BLOCK), 0)
    across = lax.broadcasted_iota(jnp.int32, (BLOCK, BLOCK), 1)
    flip = (down + across == BLOCK - 1).astype(F32).astype(BF16)
    for block in range(LEN // BLOCK):
        rows = pl.ds(block * BLOCK, BLOCK)
        width = LEN + (block + 1) * BLOCK
        first_far = 2 * LEN - width
        above = grad_out[rows, :]
        low = probs[rows, :width]
        grad_probs = dot(above, values[:width, :], 1, 1)
        inner = jnp.sum(above.astype(F32) * attended[rows, :], axis=1, keepdims=True)
        grad_scores = (low.astype(F32) * ((grad_probs - inner) * SCALE)).astype(BF16)
        grad_u = dot(grad_scores, keys[:width, :], 1, 0)
        key_sum[:width, :] += dot(grad_scores, qu[rows, :], 0, 0)
        value_sum[:width, :] += dot(low, above, 0, 0)
        far = pltpu.roll(dot(flip, grad_scores), 0, 1, stride=1, stride_axis=0).astype(BF16)
        turned = dot(flip, far).astype(BF16)
        grad_v = dot(turned, far_rel[first_far:, :], 1, 0)
        far_sum[first_far:, :] += dot(turned, qv[rows, :], 0, 0)
        grad_query[rows, :] = (grad_u + grad_v).astype(BF16)
        sum_u += jnp.sum(grad_u, axis=0, keepdims=True)
        sum_v += jnp.sum(grad_v, axis=0, keepdims=True)
    sums[0:1, :] = sum_u
    sums[1:2, :] = sum_v
    grad_far[...] = far_sum[...].astype(BF16)
    for chip in range(2):
        for side in range(2):
            start = places[2 * chip + side]
            pay[chip, side] = key_sum[rows_at(start), :].astype(BF16)
            pay[chip, 2 + side] = key_sum[rows_at(start + LEN), :].astype(BF16)
            pay[chip, 4 + side] = value_sum[rows_at(start), :].astype(BF16)
            pay[chip, 6 + side] = value_sum[rows_at(start + LEN), :].astype(BF16)
            pay[chip, 8 + side] = grad_query[rows_at(start), :]


def attention_back(spot, own, peer, qu, qv, keys, values, far_rel, probs, attended):
    return local_call(
        attention_back_kernel,
        [struct((2, 10, BLOCK, SLOT)), struct((2, SLOT), F32), struct((2 * LEN, SLOT))],
        [pltpu.VMEM((LEN, SLOT), BF16)] * 2 + [pltpu.VMEM((2 * LEN, SLOT), F32)] * 3,
        smem=1,
        vmem=9,
    )(spot, own, peer, qu, qv, keys, values, far_rel, probs, attended)


def unproject_kernel(spot, own, peer, normed, experts, logits, route, grad_logit, wide, grad_part, grad_wide, grad_all, turned):
    step = pl.program_id(0)
    flat = [own[step], own[4 + step], peer[step], peer[4 + step]]
    key_heads = two_heads(spot[1], flat[0], flat[2])
    value_heads = two_heads(spot[1], flat[1], flat[3])
    token = step >= 2
    query_at = jnp.where(token, 6 + step, 8)
    query_heads = two_heads(spot[1], own[query_at], peer[query_at])
    keep = jnp.where(token, 1.0, 0.0)
    gate = jax.nn.sigmoid(logits[...])
    routes = route[...]
    rows = rows_at(step * BLOCK)
    lane = lax.broadcasted_iota(jnp.int32, (BLOCK, SLOT), 1)
    logit_sum = grad_logit[rows_at(jnp.where(token, step - 2, 0) * BLOCK), :].astype(F32) * keep
    for pair in range(2):
        for expert in range(E):
            slot = pair * E + expert
            cols = slice(slot * SLOT, (slot + 1) * SLOT)
            sig = gate[:, slot : slot + 1]
            pick = pick_of(routes, spot[0], pair, expert)
            grad_all[rows, cols] = ((sig * pick) * value_heads[pair]).astype(BF16)
            grad_gate = jnp.sum(value_heads[pair] * experts[:, cols].astype(F32), axis=1, keepdims=True)
            logit_sum += jnp.where(lane == slot, grad_gate * pick * sig * (1.0 - sig), 0.0)
        grad_all[rows, KEY_AT + pair * SLOT : KEY_AT + (pair + 1) * SLOT] = key_heads[pair].astype(BF16)
        grad_all[rows, QUERY_AT + pair * SLOT : QUERY_AT + (pair + 1) * SLOT] = (keep * query_heads[pair]).astype(BF16)
    grad_all[rows, ROUTER_AT:WIDE] = logit_sum.astype(BF16)
    grad_part[...] = dot(grad_all[rows, :], wide[...]).astype(BF16)
    turned[:, rows] = normed[...].T

    def last():
        for part in range(5):
            cols = slice(part * 384, (part + 1) * 384)
            grad_wide[:, cols] = dot(turned[...], grad_all[:, cols]).astype(BF16)

    pl.when(step == 3)(last)


def unproject(spot, own, peer, normed, experts, logits, route, grad_logit, wide):
    block = lambda width: pl.BlockSpec((BLOCK, width), lambda step: (step, 0))
    fixed = lambda *shape: pl.BlockSpec(shape, lambda step: (0,) * len(shape))
    return pl.pallas_call(
        unproject_kernel,
        grid=(4,),
        out_shape=[struct((4 * BLOCK, D)), struct((D, WIDE))],
        in_specs=[
            IN_SMEM,
            fixed(10, BLOCK, SLOT),
            fixed(10, BLOCK, SLOT),
            block(D),
            block(EXPERTS),
            block(SLOT),
            block(2 * H),
            fixed(2 * BLOCK, SLOT),
            fixed(WIDE, D),
        ],
        out_specs=[block(D), fixed(D, WIDE)],
        scratch_shapes=[pltpu.VMEM((4 * BLOCK, WIDE), BF16), pltpu.VMEM((D, 4 * BLOCK), BF16)],
        compiler_params=pltpu.CompilerParams(vmem_limit_bytes=VMEM_BYTES),
    )(spot, own, peer, normed, experts, logits, route, grad_logit, wide)


def finish_kernel(rows, grad_mine, grad_theirs, gain, grad_resid, grad_tokens, sums):
    gain_sum = jnp.zeros((1, D), F32)
    bias_sum = jnp.zeros((1, D), F32)
    for part in range(2):
        here = slice(2 * part * BLOCK, (2 * part + 1) * BLOCK)
        scaled, inverse = centered(rows[here, :].astype(F32))
        grad = grad_mine[here, :].astype(F32) + grad_theirs[part].astype(F32)
        gain_sum += jnp.sum(grad * scaled, axis=0, keepdims=True)
        bias_sum += jnp.sum(grad, axis=0, keepdims=True)
        if part == 1:
            grad_tokens[...] = grad_resid[...] + norm_back(grad, scaled, inverse, gain[...].astype(F32))
    sums[0:1, :] = gain_sum
    sums[1:2, :] = bias_sum


def finish(rows, grad_mine, grad_theirs, gain, grad_resid):
    return local_call(finish_kernel, [struct((BLOCK, D), F32), struct((8, D), F32)], vmem=5)(
        rows, grad_mine, grad_theirs, gain, grad_resid
    )


def place():
    dp = lax.axis_index("dp")
    sq = lax.axis_index("seq")
    return dict(x=dp // 8, z=(dp // 2) % 4, y=(sq // 2) * 2 + dp % 2, core=sq % 2)


def device_of(at):
    return (at["x"] * 8 + at["z"] * 2 + at["y"] % 2, (at["y"] // 2) * 2 + at["core"])


def moved(at, axis, steps):
    other = dict(at)
    other[axis] = (at[axis] + steps) % 4
    return device_of(other)


PLAIN = (("x", 4), ("z", 4), ("ylo", 2), ("yhi", 2))
SPLIT = (("xhi", 2), ("z", 4), ("ylo", 2), ("yhi", 2), ("xlo", 2))


def part_of(name, where):
    return {"hi": where // 2, "lo": where % 2}.get(name[1:], where)


def chunk_of(ref, dims, axis, where):
    return ref.at[tuple(part_of(name, where) if name[0] == axis else slice(None) for name, _ in dims)]


def without(dims, axes):
    return tuple(dim for dim in dims if dim[0][0] not in axes)


def lead_shape(dims):
    return tuple(size for _, size in dims)


def halves(width):
    one = (width // 2 + 127) // 128 * 128
    return (0, one), (one, width - one)


def each_block(lead, step):
    count = math.prod(lead)
    if not lead:
        step(Ellipsis)
        return

    def run(flat, carry):
        index = []
        for size in reversed(lead):
            index.insert(0, flat % size)
            flat = flat // size
        step(tuple(index))
        return carry

    lax.fori_loop(0, count, run, 0)


def reduce_kernel(layouts, pieces, *refs):
    count = len(layouts)
    refs = list(refs)
    take = lambda number: [refs.pop(0) for _ in range(number)]
    sources = take(count)
    (small_in,) = take(1)
    mine = take(count)
    theirs = take(sum(dims is PLAIN for dims in layouts))
    (small_out,) = take(1)
    send_sem, recv_sem, own_sem = take(3)
    totals = take(count)
    small_slots = take(4)
    at = place()
    sibling = dict(at)
    sibling["core"] = 1 - at["core"]
    sibling = device_of(sibling)
    high, low, core = at["x"] // 2, at["x"] % 2, at["core"]
    stays = (high == low) & (low == core)
    ahead, behind = dict(at), dict(at)
    ahead["x"], ahead["core"] = 2 * core + high, low
    behind["x"], behind["core"] = 2 * low + core, high
    ahead, behind = device_of(ahead), device_of(behind)
    barrier = pltpu.get_barrier_semaphore()
    greeted = [moved(at, axis, steps) for axis in "xyz" for steps in (1, 2, 3)] + [sibling]

    def greet(device):
        pl.semaphore_signal(barrier, inc=1, device_id=device, device_id_type=pl.DeviceIdType.MESH)

    for device in greeted:
        greet(device)

    def greet_far():
        greet(ahead)
        greet(behind)
        pl.semaphore_wait(barrier, len(greeted) + 2)

    pl.when(jnp.logical_not(stays))(greet_far)
    pl.when(stays)(lambda: pl.semaphore_wait(barrier, len(greeted)))
    used = [0]

    def prepared(src, dst, device):
        slot = used[0]
        used[0] += 1
        return pltpu.make_async_remote_copy(
            src_ref=src,
            dst_ref=dst,
            send_sem=send_sem.at[slot],
            recv_sem=recv_sem.at[slot],
            device_id=device,
            device_id_type=pl.DeviceIdType.MESH,
        )

    def send(src, dst, device):
        copy = prepared(src, dst, device)
        copy.start()
        return copy

    def added(target, *terms):
        def add(index):
            total = terms[0][index].astype(F32)
            for term in terms[1:]:
                total += term[index].astype(F32)
            target[index] = total.astype(target.dtype)

        return add

    current = [sources[array].at[..., pl.ds(start, width)] for array, start, width, order in pieces]
    small_now = small_in
    open_sends = []
    for phase in range(3):
        plans = []
        for number, (array, start, width, order) in enumerate(pieces):
            axis = order[phase]
            dims = without(layouts[array], order[:phase])
            left = lead_shape(without(dims, axis))
            cols = [pl.ds(*half) for half in halves(width)]
            bufs = take(6)
            after = take(1)[0] if phase < 2 else totals[array].at[:, pl.ds(start, width)]
            near = [chunk_of(current[number], dims, axis, (at[axis] + steps) % 4) for steps in range(4)]
            plans.append((axis, left, cols, bufs, after, near, []))
        for axis, left, cols, bufs, after, near, made in plans:
            for side, steps in ((0, 1), (1, 3)):
                made.append(send(near[2].at[..., cols[side]], bufs[side], moved(at, axis, steps)))
        small_axis = "xyz"[phase]
        slots = small_slots[phase]
        small_copies = []
        slots[at[small_axis]] = small_now[...]
        for steps in (1, 2, 3):
            small_copies.append(
                send(slots.at[at[small_axis]], slots.at[at[small_axis]], moved(at, small_axis, steps))
            )
        for axis, left, cols, bufs, after, near, made in plans:
            for side, steps in ((0, 1), (1, 3)):
                made.append(
                    send(near[steps].at[..., cols[1 - side]], bufs[2 + side], moved(at, axis, steps))
                )
        for axis, left, cols, bufs, after, near, made in plans:
            for side, steps in ((0, 1), (1, 3)):
                made[side].wait_recv()
                each_block(left, added(bufs[side], bufs[side], near[steps].at[..., cols[side]]))
                made.append(send(bufs[side], bufs[4 + side], moved(at, axis, steps)))
        for copy in small_copies:
            copy.wait_recv()
        small_total = (slots[0] + slots[1]) + (slots[2] + slots[3])
        small_now = small_slots[3].at[core] if phase == 2 else small_out
        small_now[...] = small_total
        open_sends += small_copies
        current = []
        for axis, left, cols, bufs, after, near, made in plans:
            for copy in made[2:]:
                copy.wait_recv()
            for side in (0, 1):
                each_block(
                    left,
                    added(
                        after.at[..., cols[side]],
                        near[0].at[..., cols[side]],
                        bufs[4 + side],
                        bufs[3 - side],
                    ),
                )
            open_sends += made
            current.append(after)
    last = []
    pair = small_slots[3]
    last.append(send(pair.at[core], pair.at[core], sibling))
    spare = list(theirs)
    for array, dims in enumerate(layouts):
        if dims is PLAIN:
            half = totals[array].shape[0] // 2
            other = pl.ds(pl.multiple_of((1 - core) * half, 8), half)
            last.append(send(totals[array].at[other], spare.pop(0), sibling))
            mine[array][...] = totals[array][pl.ds(pl.multiple_of(core * half, 8), half), :]
            continue
        away = prepared(totals[array], mine[array], ahead)
        here = pltpu.make_async_copy(totals[array], mine[array], own_sem)
        pl.when(jnp.logical_not(stays))(away.start)
        pl.when(stays)(here.start)
        pl.when(jnp.logical_not(stays))(away.wait)
        pl.when(stays)(here.wait)
    for copy in last:
        copy.wait_recv()
    small_out[...] = pair[0] + pair[1]
    for copy in open_sends + last:
        copy.wait_send()


def reduce_all(arrays, layouts, pieces, small):
    shapes = [array.shape[1:] for array in arrays]
    arrays = [
        array.reshape(lead_shape(dims) + shape) for array, dims, shape in zip(arrays, layouts, shapes)
    ]
    scratch = []
    copies = 0
    for phase in range(3):
        for array, start, width, order in pieces:
            left = lead_shape(without(layouts[array], order[: phase + 1]))
            rows = shapes[array][0]
            (_, one), (_, two) = halves(width)
            for size in (one, two, two, one, one, two):
                scratch.append(pltpu.VMEM(left + (rows, size), BF16))
            if phase < 2:
                scratch.append(pltpu.VMEM(left + (rows, width), BF16))
            copies += 6
    copies += 9 + len(arrays) + 1
    head = [pltpu.SemaphoreType.DMA((copies,)), pltpu.SemaphoreType.DMA((copies,)), pltpu.SemaphoreType.DMA]
    head += [pltpu.VMEM(shape, F32) for shape in shapes]
    head += [pltpu.VMEM((4,) + small.shape, F32)] * 3 + [pltpu.VMEM((2,) + small.shape, F32)]
    outs = []
    for shape, dims in zip(shapes, layouts):
        outs.append(struct((shape[0] // 2 if dims is PLAIN else shape[0], shape[1]), F32))
    outs += [out for out, dims in zip(outs, layouts) if dims is PLAIN]
    outs.append(struct(small.shape, F32))
    return pl.pallas_call(
        partial(reduce_kernel, layouts, pieces),
        out_shape=outs,
        in_specs=[IN_VMEM] * (len(arrays) + 1),
        out_specs=[IN_VMEM] * len(outs),
        scratch_shapes=head + scratch,
        compiler_params=pltpu.CompilerParams(
            collective_id=0, has_side_effects=True, vmem_limit_bytes=VMEM_BYTES
        ),
    )(*arrays, small)


def sinus_far():
    frequency = jnp.exp(jnp.arange(D // 2, dtype=jnp.int32).astype(F32) * (-2.0 * math.log(10000.0) / D))
    coarse = (64 * (31 - jnp.arange(32, dtype=jnp.int32))).astype(F32)[:, None] * frequency
    fine = (63 - jnp.arange(64, dtype=jnp.int32)).astype(F32)[:, None] * frequency
    sin_a, cos_a = jnp.sin(coarse)[:, None], jnp.cos(coarse)[:, None]
    sin_b, cos_b = jnp.sin(fine)[None], jnp.cos(fine)[None]
    sines = sin_a * cos_b + cos_a * sin_b
    cosines = cos_a * cos_b - sin_a * sin_b
    return jnp.concatenate([sines, cosines], axis=2).reshape(2 * LEN, D).astype(BF16)


def swap(value):
    return lax.ppermute(value, "seq", [(0, 1), (1, 0), (2, 3), (3, 2)])


def cross(value):
    return lax.ppermute(value, "seq", [(0, 2), (2, 0), (1, 3), (3, 1)])


def body(
    tokens,
    memory,
    cotangent,
    mem_len,
    value_route,
    output_route,
    attn_norm_gain,
    attn_norm_bias,
    query_weight,
    key_weight,
    rel_weight,
    bias_u,
    bias_v,
    value_router,
    value_weight,
    out_router,
    out_weight,
    ffn_norm_gain,
    ffn_norm_bias,
    up_weight,
    up_bias,
    down_weight,
    down_bias,
):
    seq_index = lax.axis_index("seq")
    core, chip = seq_index % 2, seq_index // 2
    spot = jnp.stack([core, chip, mem_len[0]]).astype(jnp.int32)
    row = lambda vector: vector.reshape(1, -1)
    tokens, memory, cotangent = tokens[0], memory[0], cotangent[0]
    routes = jnp.concatenate(
        [value_route[0].reshape(2 * BLOCK, 2 * H), output_route[0].reshape(BLOCK, 2 * H)], axis=0
    )
    memory_theirs, tokens_theirs, routes_theirs = swap(memory), swap(tokens), swap(routes)
    cot = jnp.concatenate([cotangent, swap(cotangent)], axis=0)
    rows = jnp.concatenate([memory, memory_theirs, tokens, tokens_theirs], axis=0)
    value_routes = jnp.stack(
        [routes[: 2 * BLOCK].reshape(2, BLOCK, 2 * H), routes_theirs[: 2 * BLOCK].reshape(2, BLOCK, 2 * H)], axis=1
    ).reshape(4 * BLOCK, 2 * H)
    out_routes = jnp.concatenate([routes[2 * BLOCK :], routes_theirs[2 * BLOCK :]], axis=0)
    wide, rel, out_wide = prepare(
        spot, value_weight, key_weight, query_weight, rel_weight, value_router, out_router, out_weight
    )
    head_bias = lambda bias: jnp.pad(
        lax.dynamic_slice_in_dim(bias.astype(F32), seq_index * DH, DH, 0), (0, SLOT - DH)
    ).reshape(1, SLOT)
    sinus = sinus_far()
    far_rel = dot(sinus, rel, 1, 1).astype(BF16)
    attn_gain = row(attn_norm_gain)
    normed, experts, logits, pay = project(spot, rows, attn_gain, row(attn_norm_bias), wide, value_routes)
    pay_own = jnp.where(chip == 0, pay[0], pay[1])
    pay_peer = cross(jnp.where(chip == 0, pay[1], pay[0]))
    attended, probs, keys, values, qu, qv, back = attention(
        spot, pay_own, pay_peer, head_bias(bias_u), head_bias(bias_v), far_rel
    )
    att_own, att_peer = back[:2], cross(back[2:])
    mixed, out_part = mix(spot, att_own, att_peer, logits, out_routes, out_wide)
    resid, final_mine, final_theirs, norm_part, grad_up, grad_up_bias, grad_down = feed(
        spot,
        rows,
        out_part,
        swap(out_part),
        cot,
        row(ffn_norm_gain),
        row(ffn_norm_bias),
        up_weight,
        row(up_bias),
        down_weight,
        row(down_bias),
    )
    grad_resid, grad_att, grad_out_logit, grad_out, feed_sums, result = unmix(
        spot,
        resid,
        norm_part,
        swap(norm_part),
        cot,
        row(ffn_norm_gain),
        att_own,
        att_peer,
        mixed,
        logits,
        out_routes,
        out_wide,
        final_mine,
        swap(final_theirs),
    )
    pay_back, bias_sums, grad_far = attention_back(
        spot, grad_att[0], cross(grad_att[1]), qu, qv, keys, values, far_rel, probs, attended
    )
    grad_rel = dot(sinus, grad_far, 0, 0).astype(BF16)
    part, grad_wide = unproject(
        spot, pay_back[0], cross(pay_back[1]), normed, experts, logits, value_routes, grad_out_logit, wide
    )
    part_theirs = swap(part.reshape(2, 2, BLOCK, D)[:, 1])
    grad_tokens, attn_sums = finish(rows, part, part_theirs, attn_gain, grad_resid)
    nothing = jnp.zeros((), F32)
    up_bias_full = jnp.concatenate(
        [jnp.where(core == 0, grad_up_bias[0], nothing), jnp.where(core == 1, grad_up_bias[0], nothing)]
    )
    narrow = jnp.concatenate(
        [attn_sums[:2].T, feed_sums[:3].T, up_bias_full.reshape(D, 4), jnp.zeros((D, SLOT - 9), F32)], axis=1
    ).astype(BF16)
    blank = jnp.zeros((), BF16)
    rest = jnp.concatenate(
        [jnp.where(chip == 0, grad_rel, blank), jnp.where(chip == 1, grad_rel, blank), narrow], axis=1
    )
    picks = jnp.arange(E, dtype=jnp.int32)
    chosen = (routes.reshape(3 * BLOCK, H, 2)[..., None] == picks).astype(F32).sum(axis=2)
    counts = jnp.concatenate(
        [chosen[: 2 * BLOCK].sum(axis=0).reshape(-1), chosen[2 * BLOCK :].sum(axis=0).reshape(-1)]
    )
    head_at = (jnp.arange(H) == seq_index).astype(F32)[:, None]
    small = jnp.concatenate(
        [
            head_at * bias_sums[0:1],
            head_at * bias_sums[1:2],
            jnp.pad(counts, (0, SLOT - 40)).reshape(1, SLOT),
            jnp.zeros((7, SLOT), F32),
        ],
        axis=0,
    )
    pieces = (
        (0, 0, 2048, "xyz"),
        (1, 0, 1024, "yzx"),
        (2, 0, 1408, "zxy"),
        (3, 0, 768, "zxy"),
        (4, 0, 384, "zxy"),
        (2, 1408, 512, "xyz"),
        (3, 768, 512, "yzx"),
    )
    layouts = (PLAIN, SPLIT, PLAIN, PLAIN, PLAIN)
    up_mine, down_mine, wide_mine, out_mine, rest_mine, up_their, wide_their, out_their, rest_their, small_sum = (
        reduce_all(
            [
                grad_up.reshape(64, 16, FF // 2),
                grad_down.reshape(64, 32, D),
                grad_wide.reshape(64, 16, WIDE),
                grad_out.reshape(64, 16, EXPERTS),
                rest.reshape(64, 16, 3 * SLOT),
            ],
            layouts,
            pieces,
            small,
        )
    )
    first = core == 0

    def cores(mine, theirs):
        return jnp.stack([jnp.where(first, mine, theirs), jnp.where(first, theirs, mine)])

    def by_head(both, parts, width):
        shaped = both.reshape(2, 8, 2, parts, -1)[..., :width]
        return shaped.transpose(1, 2, 0, 3, 4).reshape(8, H * parts * width)

    wide_both = cores(wide_mine, wide_their)
    out_both = cores(out_mine, out_their)
    rest_both = cores(rest_mine, rest_their)
    narrow_sum = rest_mine[:, 2 * SLOT :] + rest_their[:, 2 * SLOT :]
    up_both = cores(up_mine, up_their)
    per_head = lambda rows: rows[:, :DH].reshape(H * DH)
    return (
        result[None],
        grad_tokens[None],
        narrow_sum[:, 0],
        narrow_sum[:, 1],
        by_head(wide_both[..., QUERY_AT:ROUTER_AT], 1, DH),
        by_head(wide_both[..., KEY_AT:QUERY_AT], 1, DH),
        by_head(rest_both[..., : 2 * SLOT], 1, DH),
        per_head(small_sum[:4]),
        per_head(small_sum[4:8]),
        by_head(wide_both[..., ROUTER_AT : ROUTER_AT + 10], E, 1),
        by_head(wide_both[..., :EXPERTS], E, DH),
        by_head(wide_both[..., ROUTER_AT + 10 : ROUTER_AT + 20], E, 1),
        by_head(out_both, E, DH).T,
        narrow_sum[:, 2],
        narrow_sum[:, 3],
        jnp.concatenate([up_both[0], up_both[1]], axis=1),
        narrow_sum[:, 5:9].reshape(-1),
        down_mine,
        narrow_sum[:, 4],
        jnp.round(small_sum[8, :40]).astype(jnp.int32).reshape(2, H, E),
    )


def solution(mesh):
    in_specs = (
        P("dp", "seq", None),
        P("dp", "seq", None),
        P("dp", "seq", None),
        P("dp"),
        P("dp", None, "seq", None, None),
        P("dp", "seq", None, None),
        P(),
        P(),
        P(),
        P(),
        P(),
        P(),
        P(),
        P(),
        P(),
        P(),
        P(),
        P(),
        P(),
        P(),
        P(),
        P(),
        P(),
    )
    out_specs = (
        P("dp", "seq", None),
        P("dp", "seq", None),
        P(("dp", "seq")),
        P(("dp", "seq")),
        P(("dp", "seq"), None),
        P(("dp", "seq"), None),
        P(("dp", "seq"), None),
        P(),
        P(),
        P(("dp", "seq"), None),
        P(("dp", "seq"), None),
        P(("dp", "seq"), None),
        P(None, ("dp", "seq")),
        P(("dp", "seq")),
        P(("dp", "seq")),
        P(("dp", "seq"), None),
        P(("dp", "seq")),
        P(("dp", "seq"), None),
        P(("dp", "seq")),
        P(),
    )
    return jax.shard_map(body, mesh=mesh, in_specs=in_specs, out_specs=out_specs, check_vma=False)
```

time: 5490 us -> 327 us (0.06); the launches traced: 5390 us -> 323 us
  waiting for transfers between devices: 4480 us -> 32.1 us
  local copies, waits for them, and re-layouts: 632 us -> 39.1 us
  Pallas kernels: 0 us -> 212 us
  matrix products: 152 us -> 3.54 us
  blocking collectives: 68 us -> 0 us
    reduce_scatter x9 -> x0, waiting for transfers between devices: 4470 us -> none  [the longest x1 670 us: body(): lax.psum_scatter(grad_up, ('dp', 'seq'), scatter_dimension=0, tiled=True)]
    unnamed x206 -> x50, local copies, waits for them, and re-layouts: 446 us -> 8.4 us
    pallas_call x0 -> x10, Pallas kernels: none -> 212 us  [the longest x1 91.4 us: reduce_all(): pl.pallas_call(partial(reduce_kernel, layouts, pieces), out_shape=outs, i...]
    dot_general x35 -> x2, matrix products: 152 us -> 3.54 us  [dot(): lax.dot_general(left, right, (((left_dim,), (right_dim,)), ((), ())), pre...]
    unnamed x1 -> x0, blocking collectives: 68 us -> none
  transfers between devices with their start and end apart: 13 -> 12, of which waited for: 8 -> 6; matrix products, arithmetic and copies ran while one was open for 8% -> 7% of each run, Pallas kernels for 0% -> 2%
where the time goes in v1:
time: 327 us; the launch traced here: 323 us
  Pallas kernels  212 us (65%)
  local copies, waits for them, and re-layouts  39.1 us (12%)
  waiting for transfers between devices  32.1 us (10%)
  starting transfers between devices  18.2 us (6%)
  other arithmetic  15.5 us (5%)
  matrix products  3.54 us (1%)
    pallas_call x1, Pallas kernels, reduce_all(): pl.pallas_call(partial(reduce_kernel, layouts, pieces), out_shape=outs, i...  91.4 us
    ppermute x4, waiting for transfers between devices, cross(): return lax.ppermute(value, 'seq', [(0, 2), (2, 0), (1, 3), (3, 1)])  28.5 us
    pallas_call x1, Pallas kernels, unproject(): pl.pallas_call(unproject_kernel, grid=(4,), out_shape=[struct((4 * BLOCK,...  28.3 us
    pallas_call x1, Pallas kernels, feed(): pl.pallas_call(feed_kernel, grid_spec=pltpu.PrefetchScalarGridSpec(num_sc...  24 us
    pallas_call x1, Pallas kernels, project(): pl.pallas_call(project_kernel, grid=(4,), out_shape=[struct((4 * BLOCK, D...  13.5 us
    pallas_call x1, Pallas kernels, unmix(): local_call(unmix_kernel, [struct((BLOCK, D), F32), struct((2, 2, BLOCK, S...  13.3 us
    pallas_call x1, Pallas kernels, attention_back(): local_call(attention_back_kernel, [struct((2, 10, BLOCK, SLOT)), struct((...  13 us
    ppermute x4, starting transfers between devices, cross(): return lax.ppermute(value, 'seq', [(0, 2), (2, 0), (1, 3), (3, 1)])  12.2 us
  transfers between devices with their start and end apart: 12, of which 6 were waited for; matrix products, arithmetic and copies ran while one was open for 7% of the time, Pallas kernels for 2%

profile of v1, /device:TPU:3, one launch (start us, length us, event | category | flops | bytes accessed | tf_op | source)
XLA Modules:
  0.0 322.5 jit_solution(12084370630951712039)
XLA Ops:
  8.5 1.3 reshape.301.gain
  11.0 7.7 %shard_map.374 = (bf16[1920,1024]{1,0:T(8,128)(2,1)}, bf16[128,1024]{1,0:T(8,128)(2,1)}, bf16[1280,1024]{1,0:T(8,128)(2,1)}) custom-call(s32[3]{0:T(128)} %pad_add_fusion.4.spot, bf16[2240,1024]{1,0:T(8,128)(2,1)} %bitcast.119, bf16[448,1024]{1,0:T(8,128)(2,1)} %bitcast.129, bf16[448,1024]{1,0:T(8,128)(2,1)} %bitcast.130, bf16[448,1024]{1,0:T(8,128)(2,1)} %bitcast.131, ...), custom_call_target="tpu_custom_call" | custom-call | tf_op jit(solution)/shard_map/pallas_call | solution.py:112
  19.7 1.6 pad_maximum_fusion.5.rows
  21.3 13.5 %shard_map.375 = (bf16[1024,1024]{1,0:T(8,128)(2,1)}, bf16[1024,1280]{1,0:T(8,128)(2,1)}, f32[1024,128]{1,0:T(8,128)}, bf16[2,10,256,128]{3,2,1,0:T(8,128)(2,1)}) custom-call(s32[3]{0:T(128)} %pad_add_fusion.4.spot, bf16[1024,1024]{1,0:T(8,128)(2,1)} %pad_maximum_fusion.5.rows, bf16[1,1024]{1,0:T(2,128)(2,1)} %reshape.301.gain, ...), custom_call_target="tpu_custom_call" | custom-call | tf_op jit(solution)/shard_map/pallas_call | solution.py:146
  34.8 2.3 select_bitcast_fusion
  37.0 3.4 %collective-permute-start.3 = (bf16[10,256,128]{2,1,0:T(8,128)(2,1)S(1)}, bf16[10,256,128]{2,1,0:T(8,128)(2,1)S(1)}, u32[]{:S(2)}, u32[]{:S(2)}) collective-permute-start(bf16[10,256,128]{2,1,0:T(8,128)(2,1)S(1)} %get-tuple-element.121), channel_id=1, source_target_pairs={{0,2},{2,0},{1,3},{3,1},{4,6},{6,4},{5,7},{7,5},{8,10},{10,8},{9,1... | collective-permute-start | bytes 1966088 | tf_op jit(solution)/shard_map/ppermute | solution.py:850
  40.4 1.3 add_convert_fusion
  41.8 2.1 fusion.2.far_rel
  43.9 11.5 %collective-permute-done.3.peer = bf16[10,256,128]{2,1,0:T(8,128)(2,1)S(1)} collective-permute-done((bf16[10,256,128]{2,1,0:T(8,128)(2,1)S(1)}, bf16[10,256,128]{2,1,0:T(8,128)(2,1)S(1)}, u32[]{:S(2)}, u32[]{:S(2)}) %collective-permute-start.3) | collective-permute-done | bytes 655392 | tf_op jit(solution)/shard_map/ppermute | solution.py:850
  56.2 9.1 %shard_map.376 = (f32[1024,128]{1,0:T(8,128)}, bf16[1024,2048]{1,0:T(8,128)(2,1)}, bf16[2048,128]{1,0:T(8,128)(2,1)}, bf16[2048,128]{1,0:T(8,128)(2,1)}, bf16[10...) custom-call(s32[3]{0:T(128)} %pad_add_fusion.4.spot, ...), custom_call_target="tpu_custom_call" | custom-call | tf_op jit(solution)/shard_map/pallas_call | solution.py:205
  65.3 1.6 fusion.17
  67.0 2.8 collective-permute-start.4
  70.6 2.0 collective-permute-done.4.peer
  73.3 6.6 %shard_map.377 = (bf16[512,1280]{1,0:T(8,128)(2,1)}, bf16[512,1024]{1,0:T(8,128)(2,1)}) custom-call(s32[3]{0:T(128)} %pad_add_fusion.4.spot, bf16[2,256,128]{2,1,0:T(8,128)(2,1)} %get-tuple-element.130.own, bf16[2,256,128]{2,1,0:T(8,128)(2,1)} %copy-done.7, f32[1024,128]{1,0:T(8,128)} %get-tuple-element.70.logits, s32[512,8]{1,0:T(8,128)} %copy.106.route, ...), custom_call_target="tpu_custom_call" | custom-call | tf_op jit(solution)/shard_map/pallas_call | solution.py:240
  79.9 1.7 collective-permute-start.5
  86.7 24.0 %shard_map.378 = (f32[512,1024]{1,0:T(8,128)}, f32[256,1024]{1,0:T(8,128)}, bf16[256,1024]{1,0:T(8,128)(2,1)}, bf16[512,1024]{1,0:T(8,128)(2,1)}, bf16[1024,2048...) custom-call(s32[3]{0:T(128)} %pad_add_fusion.4.spot, bf16[1024,1024]{1,0:T(8,128)(2,1)} %pad_maximum_fusion.5.rows, ...), custom_call_target="tpu_custom_call" | custom-call | tf_op jit(solution)/shard_map/pallas_call | solution.py:308
  111.3 3.2 collective-permute-done.8.final_theirs
  115.5 13.3 %shard_map.379 = (f32[256,1024]{1,0:T(8,128)}, bf16[2,2,256,128]{3,2,1,0:T(8,128)(2,1)}, bf16[512,128]{1,0:T(8,128)(2,1)}, bf16[1024,1280]{1,0:T(8,128)(2,1)}, f...) custom-call(s32[3]{0:T(128)} %pad_add_fusion.4.spot, f32[512,1024]{1,0:T(8,128)} %get-tuple-element.73.resid, ...), custom_call_target="tpu_custom_call" | custom-call | tf_op jit(solution)/shard_map/pallas_call | solution.py:419
  128.8 1.6 slice_bitcast_fusion.3
  130.5 3.0 collective-permute-start.9
  133.5 3.4 %collective-permute-done.9.peer = bf16[2,256,128]{2,1,0:T(8,128)(2,1)S(1)} collective-permute-done((bf16[2,256,128]{2,1,0:T(8,128)(2,1)S(1)}, bf16[2,256,128]{2,1,0:T(8,128)(2,1)S(1)}, u32[]{:S(2)}, u32[]{:S(2)}) %collective-permute-start.9) | collective-permute-done | bytes 131104 | tf_op jit(solution)/shard_map/ppermute | solution.py:850
  137.5 13.0 %shard_map.380 = (bf16[2,10,256,128]{3,2,1,0:T(8,128)(2,1)}, f32[2,128]{1,0:T(2,128)}, bf16[2048,128]{1,0:T(8,128)(2,1)}) custom-call(s32[3]{0:T(128)} %pad_add_fusion.4.spot, bf16[2,256,128]{2,1,0:T(8,128)(2,1)} %get-tuple-element.128.own, bf16[2,256,128]{2,1,0:T(8,128)(2,1)} %copy-done.12, bf16[1024,128]{1,0:T(8,128)(2,1)} %get-tuple-element.80.qu, ...), custom_call_target="tpu_custom_call" | custom-call | tf_op jit(solution)/shard_map/pallas_call | solution.py:500
  150.5 2.2 slice_bitcast_fusion.1
  152.8 3.0 collective-permute-start.10
  157.9 11.7 %collective-permute-done.10.peer = bf16[10,256,128]{2,1,0:T(8,128)(2,1)S(1)} collective-permute-done((bf16[10,256,128]{2,1,0:T(8,128)(2,1)S(1)}, bf16[10,256,128]{2,1,0:T(8,128)(2,1)S(1)}, u32[]{:S(2)}, u32[]{:S(2)}) %collective-permute-start.10) | collective-permute-done | bytes 655392 | tf_op jit(solution)/shard_map/ppermute | solution.py:850
  170.4 28.3 %shard_map.381 = (bf16[1024,1024]{1,0:T(8,128)(2,1)}, bf16[1024,1920]{1,0:T(8,128)(2,1)}) custom-call(s32[3]{0:T(128)} %pad_add_fusion.4.spot, bf16[10,256,128]{2,1,0:T(8,128)(2,1)} %get-tuple-element.120.own, bf16[10,256,128]{2,1,0:T(8,128)(2,1)} %copy-done.5, bf16[1024,1024]{1,0:T(8,128)(2,1)} %get-tuple-element.87.normed, ...), custom_call_target="tpu_custom_call" | custom-call | tf_op jit(solution)/shard_map/pallas_call | solution.py:549
  198.7 1.3 slice_bitcast_fusion
  200.0 2.2 collective-permute-start.11
  203.7 1.5 broadcast_select_fusion
  206.2 5.0 %shard_map.382 = (f32[256,1024]{1,0:T(8,128)}, f32[8,1024]{1,0:T(8,128)}) custom-call(bf16[1024,1024]{1,0:T(8,128)(2,1)} %pad_maximum_fusion.5.rows, bf16[1024,1024]{1,0:T(8,128)(2,1)} %get-tuple-element.90.grad_mine, bf16[2,256,1024]{2,1,0:T(8,128)(2,1)} %copy-done.3, bf16[1,1024]{1,0:T(2,128)(2,1)} %reshape.301.gain, f32[256,1024]{1,0:T(8,128)} %get-tuple-element.91.grad_resid), custom_call_target="tpu_custom_call" | custom-call | tf_op jit(solution)/shard_map/pallas_call | solution.py:586
  214.0 91.4 %shard_map.383 = (f32[8,2048]{1,0:T(8,128)}, f32[32,1024]{1,0:T(8,128)}, f32[8,1920]{1,0:T(8,128)}, f32[8,1280]{1,0:T(8,128)}, f32[8,384]{1,0:T(8,128)}, /*index...) custom-call(bf16[4,4,2,2,16,2048]{5,4,3,2,1,0:T(8,128)(2,1)} %bitcast.120, ...), custom_call_target="tpu_custom_call" | custom-call | tf_op jit(solution)/shard_map/pallas_call | solution.py:822
  320.5 1.6 copy.135
  (153 shorter events, 42.3 us)
Async XLA Ops:
  0.7 19.1 %collective-permute-start = (bf16[256,1024]{1,0:T(8,128)(2,1)}, bf16[256,1024]{1,0:T(8,128)(2,1)S(1)}, u32[]{:S(2)}, u32[]{:S(2)}) collective-permute-start(bf16[256,1024]{1,0:T(8,128)(2,1)} %bitcast.137), channel_id=1, source_target_pairs={{0,1},{1,0},{2,3},{3,2},{4,5},{5,4},{6,7},{7,6},{8,9},{9,8},{10,11... | collective-permute-start | bytes 1572872 | tf_op jit(solution)/shard_map/ppermute | solution.py:846
  1.4 18.3 %collective-permute-start.1 = (bf16[256,1024]{1,0:T(8,128)(2,1)}, bf16[256,1024]{1,0:T(8,128)(2,1)S(1)}, u32[]{:S(2)}, u32[]{:S(2)}) collective-permute-start(bf16[256,1024]{1,0:T(8,128)(2,1)} %bitcast.135), channel_id=1, source_target_pairs={{0,1},{1,0},{2,3},{3,2},{4,5},{5,4},{6,7},{7,6},{8,9},{9,8},{10,11... | collective-permute-start | bytes 1572872 | tf_op jit(solution)/shard_map/ppermute | solution.py:846
  3.0 15.8 %collective-permute-start.2 = (s32[768,8]{0,1:T(8,128)S(1)}, s32[768,8]{0,1:T(8,128)S(1)}, u32[]{:S(2)}, u32[]{:S(2)}) collective-permute-start(s32[768,8]{0,1:T(8,128)S(1)} %pad_add_fusion.1), channel_id=1, source_target_pairs={{0,1},{1,0},{2,3},{3,2},{4,5},{5,4},{6,7},{7,6},{8,9},{9,8},{10,11... | collective-permute-start | bytes 73736 | tf_op jit(solution)/shard_map/ppermute | solution.py:846
  11.0 8.7 %copy-start.9 = (bf16[1,256,1024]{2,1,0:T(8,128)(2,1)S(1)}, bf16[1,256,1024]{2,1,0:T(8,128)(2,1)}, u32[]{:S(2)}) copy-start(bf16[1,256,1024]{2,1,0:T(8,128)(2,1)} %param.23) | copy-start | bytes 1572868
  11.0 8.7 %copy-start.10 = (bf16[1,256,1024]{2,1,0:T(8,128)(2,1)S(1)}, bf16[1,256,1024]{2,1,0:T(8,128)(2,1)}, u32[]{:S(2)}) copy-start(bf16[1,256,1024]{2,1,0:T(8,128)(2,1)} %param.24) | copy-start | bytes 1572868
  34.8 7.0 %copy-start.22 = (bf16[128,1024]{1,0:T(8,128)(2,1)S(1)}, bf16[128,1024]{1,0:T(8,128)(2,1)}, u32[]{:S(2)}) copy-start(bf16[128,1024]{1,0:T(8,128)(2,1)} %get-tuple-element.68) | copy-start | bytes 786436
  37.0 18.3 %collective-permute-start.3 = (bf16[10,256,128]{2,1,0:T(8,128)(2,1)S(1)}, bf16[10,256,128]{2,1,0:T(8,128)(2,1)S(1)}, u32[]{:S(2)}, u32[]{:S(2)}) collective-permute-start(bf16[10,256,128]{2,1,0:T(8,128)(2,1)S(1)} %get-tuple-element.121), channel_id=1, source_target_pairs={{0,2},{2,0},{1,3},{3,1},{4,6},{6,4},{5,7},{7,5},{8,10},{10,8},{9,1... | collective-permute-start | bytes 1966088 | tf_op jit(solution)/shard_map/ppermute | solution.py:850
  41.8 2.1 copy-start
  43.9 37.8 %copy-start.8 = (bf16[1,256,1024]{2,1,0:T(8,128)(2,1)S(1)}, bf16[1,256,1024]{2,1,0:T(8,128)(2,1)}, u32[]{:S(2)}) copy-start(bf16[1,256,1024]{2,1,0:T(8,128)(2,1)} %param.25) | copy-start | bytes 1572868
  43.9 38.0 %copy-start.16 = (bf16[1024]{0:T(1024)(128)(2,1)S(1)}, bf16[1024]{0:T(1024)(128)(2,1)}, u32[]{:S(2)}) copy-start(bf16[1024]{0:T(1024)(128)(2,1)} %param.40) | copy-start | bytes 6148
  43.9 38.6 %copy-start.14 = (bf16[4096]{0:T(1024)(128)(2,1)S(1)}, bf16[4096]{0:T(1024)(128)(2,1)}, u32[]{:S(2)}) copy-start(bf16[4096]{0:T(1024)(128)(2,1)} %param.43) | copy-start | bytes 24580
  43.9 39.2 %copy-start.17 = (bf16[1024]{0:T(1024)(128)(2,1)S(1)}, bf16[1024]{0:T(1024)(128)(2,1)}, u32[]{:S(2)}) copy-start(bf16[1024]{0:T(1024)(128)(2,1)} %param.41) | copy-start | bytes 6148
  43.9 39.8 %copy-start.18 = (bf16[1024]{0:T(1024)(128)(2,1)S(1)}, bf16[1024]{0:T(1024)(128)(2,1)}, u32[]{:S(2)}) copy-start(bf16[1024]{0:T(1024)(128)(2,1)} %param.45) | copy-start | bytes 6148
  67.0 5.7 %collective-permute-start.4 = (bf16[2,256,128]{2,1,0:T(8,128)(2,1)S(1)}, bf16[2,256,128]{2,1,0:T(8,128)(2,1)S(1)}, u32[]{:S(2)}, u32[]{:S(2)}) collective-permute-start(bf16[2,256,128]{2,1,0:T(8,128)(2,1)S(1)} %get-tuple-element.129), channel_id=1, source_target_pairs={{0,2},{2,0},{1,3},{3,1},{4,6},{6,4},{5,7},{7,5},{8,10},{10,8},{9,1... | collective-permute-start | bytes 393224 | tf_op jit(solution)/shard_map/ppermute | solution.py:850
  79.9 5.8 %collective-permute-start.5 = (bf16[512,1024]{1,0:T(8,128)(2,1)}, bf16[512,1024]{1,0:T(8,128)(2,1)S(1)}, u32[]{:S(2)}, u32[]{:S(2)}) collective-permute-start(bf16[512,1024]{1,0:T(8,128)(2,1)} %get-tuple-element.72.part_mine), channel_id=1, source_target_pairs={{0,1},{1,0},{2,3},{3,2},{4,5},{5,4},{6,7},{7,6},{8,9},{9,8},{10,11... | collective-permute-start | bytes 3145736 | tf_op jit(solution)/shard_map/ppermute | solution.py:846
  81.6 3.0 collective-permute-start.6
  85.7 1.0 copy-start.2
  110.8 3.8 %collective-permute-start.7 = (bf16[512,1024]{1,0:T(8,128)(2,1)}, bf16[512,1024]{1,0:T(8,128)(2,1)S(1)}, u32[]{:S(2)}, u32[]{:S(2)}) collective-permute-start(bf16[512,1024]{1,0:T(8,128)(2,1)} %get-tuple-element.74.grad_mine), channel_id=1, source_target_pairs={{0,1},{1,0},{2,3},{3,2},{4,5},{5,4},{6,7},{7,6},{8,9},{9,8},{10,11... | collective-permute-start | bytes 3145736 | tf_op jit(solution)/shard_map/ppermute | solution.py:846
  111.2 3.4 %collective-permute-start.8 = (bf16[256,1024]{1,0:T(8,128)(2,1)}, bf16[256,1024]{1,0:T(8,128)(2,1)}, u32[]{:S(2)}, u32[]{:S(2)}) collective-permute-start(bf16[256,1024]{1,0:T(8,128)(2,1)} %get-tuple-element.77), channel_id=1, source_target_pairs={{0,1},{1,0},{2,3},{3,2},{4,5},{5,4},{6,7},{7,6},{8,9},{9,8},{10,11... | collective-permute-start | bytes 1572872 | tf_op jit(solution)/shard_map/ppermute | solution.py:846
  114.6 1.0 copy-start.4
  115.5 17.9 %copy-start.13 = (s32[1,256,4,2]{1,3,2,0:T(2,128)S(1)}, s32[1,256,4,2]{1,3,2,0:T(2,128)}, u32[]{:S(2)}) copy-start(s32[1,256,4,2]{1,3,2,0:T(2,128)} %param.28) | copy-start | bytes 24580
  130.5 6.4 %collective-permute-start.9 = (bf16[2,256,128]{2,1,0:T(8,128)(2,1)S(1)}, bf16[2,256,128]{2,1,0:T(8,128)(2,1)S(1)}, u32[]{:S(2)}, u32[]{:S(2)}) collective-permute-start(bf16[2,256,128]{2,1,0:T(8,128)(2,1)S(1)} %get-tuple-element.127), channel_id=1, source_target_pairs={{0,2},{2,0},{1,3},{3,1},{4,6},{6,4},{5,7},{7,5},{8,10},{10,8},{9,1... | collective-permute-start | bytes 393224 | tf_op jit(solution)/shard_map/ppermute | solution.py:850
  137.5 19.4 %copy-start.15 = (f32[1,2048]{1,0:T(1,128)S(1)}, f32[1,2048]{1,0:T(1,128)}, u32[]{:S(2)}) copy-start(f32[1,2048]{1,0:T(1,128)} %get-tuple-element.100) | copy-start | bytes 24580
  152.8 16.8 %collective-permute-start.10 = (bf16[10,256,128]{2,1,0:T(8,128)(2,1)S(1)}, bf16[10,256,128]{2,1,0:T(8,128)(2,1)S(1)}, u32[]{:S(2)}, u32[]{:S(2)}) collective-permute-start(bf16[10,256,128]{2,1,0:T(8,128)(2,1)S(1)} %get-tuple-element.119), channel_id=1, source_target_pairs={{0,2},{2,0},{1,3},{3,1},{4,6},{6,4},{5,7},{7,5},{8,10},{10,8},{9,1... | collective-permute-start | bytes 1966088 | tf_op jit(solution)/shard_map/ppermute | solution.py:850
  169.5 0.9 copy-start.5
  170.4 32.6 %copy-start.19 = (f32[2,128]{1,0:T(2,128)S(1)}, f32[2,128]{1,0:T(2,128)}, u32[]{:S(2)}) copy-start(f32[2,128]{1,0:T(2,128)} %get-tuple-element.101) | copy-start | bytes 3076
  170.4 32.7 %copy-start.20 = (f32[1,128]{1,0:T(1,128)S(1)}, f32[1,128]{1,0:T(1,128)}, u32[]{:S(2)}) copy-start(f32[1,128]{1,0:T(1,128)} %fusion.14) | copy-start | bytes 1540
  170.4 33.3 %copy-start.1 = (bf16[32,64,512]{2,1,0:T(8,128)(2,1)S(1)}, bf16[32,64,512]{2,1,0:T(8,128)(2,1)}, u32[]{:S(2)}) copy-start(bf16[32,64,512]{2,1,0:T(8,128)(2,1)} %copy-done) | copy-start | bytes 6291460
  170.4 33.3 %copy-start.21 = (bf16[2048,128]{1,0:T(8,128)(2,1)S(1)}, bf16[2048,128]{1,0:T(8,128)(2,1)}, u32[]{:S(2)}) copy-start(bf16[2048,128]{1,0:T(8,128)(2,1)} %get-tuple-element.97) | copy-start | bytes 1572868
  200.0 5.2 %collective-permute-start.11 = (bf16[2,256,1024]{2,1,0:T(8,128)(2,1)S(1)}, bf16[2,256,1024]{2,1,0:T(8,128)(2,1)S(1)}, u32[]{:S(2)}, u32[]{:S(2)}) collective-permute-start(bf16[2,256,1024]{2,1,0:T(8,128)(2,1)S(1)} %slice_bitcast_fusion), channel_id=1, source_target_pairs={{0,1},{1,0},{2,3},{3,2},{4,5},{5,4},{6,7},{7,6},{8,9},{9,8},{10,11... | collective-permute-start | bytes 3145736 | tf_op jit(solution)/shard_map/ppermute | solution.py:846
  205.2 6.9 %copy-start.11 = (bf16[1024,128]{0,1:T(8,128)(2,1)S(1)}, bf16[1024,128]{0,1:T(8,128)(2,1)}, u32[]{:S(2)}) copy-start(bf16[1024,128]{0,1:T(8,128)(2,1)} %get-tuple-element.126) | copy-start | bytes 786436
  205.2 1.0 copy-start.3
  (3 other events, 2.2 us)

commit v2 on v1

--- a/solution.py
+++ b/solution.py
@@ -432,80 +432,6 @@
     )(spot, resid, grad_mine, grad_theirs, cot, gain, own, peer, mixed, logits, route, out_wide, final_mine, final_theirs)
 
 
-def attention_back_kernel(
-    spot,
-    own,
-    peer,
-    qu,
-    qv,
-    keys,
-    values,
-    far_rel,
-    probs,
-    attended,
-    pay,
-    sums,
-    grad_far,
-    grad_out,
-    grad_query,
-    key_sum,
-    value_sum,
-    far_sum,
-):
-    places = spots_of(spot[0], spot[1])
-    for chip, given in ((0, own), (1, peer)):
-        for side in range(2):
-            grad_out[rows_at(places[2 * chip + side]), :] = given[side]
-    key_sum[...] = jnp.zeros_like(key_sum)
-    value_sum[...] = jnp.zeros_like(value_sum)
-    far_sum[...] = jnp.zeros_like(far_sum)
-    sum_u = jnp.zeros((1, SLOT), F32)
-    sum_v = jnp.zeros((1, SLOT), F32)
-    down = lax.broadcasted_iota(jnp.int32, (BLOCK, BLOCK), 0)
-    across = lax.broadcasted_iota(jnp.int32, (BLOCK, BLOCK), 1)
-    flip = (down + across == BLOCK - 1).astype(F32).astype(BF16)
-    for block in range(LEN // BLOCK):
-        rows = pl.ds(block * BLOCK, BLOCK)
-        width = LEN + (block + 1) * BLOCK
-        first_far = 2 * LEN - width
-        above = grad_out[rows, :]
-        low = probs[rows, :width]
-        grad_probs = dot(above, values[:width, :], 1, 1)
-        inner = jnp.sum(above.astype(F32) * attended[rows, :], axis=1, keepdims=True)
-        grad_scores = (low.astype(F32) * ((grad_probs - inner) * SCALE)).astype(BF16)
-        grad_u = dot(grad_scores, keys[:width, :], 1, 0)
-        key_sum[:width, :] += dot(grad_scores, qu[rows, :], 0, 0)
-        value_sum[:width, :] += dot(low, above, 0, 0)
-        far = pltpu.roll(dot(flip, grad_scores), 0, 1, stride=1, stride_axis=0).astype(BF16)
-        turned = dot(flip, far).astype(BF16)
-        grad_v = dot(turned, far_rel[first_far:, :], 1, 0)
-        far_sum[first_far:, :] += dot(turned, qv[rows, :], 0, 0)
-        grad_query[rows, :] = (grad_u + grad_v).astype(BF16)
-        sum_u += jnp.sum(grad_u, axis=0, keepdims=True)
-        sum_v += jnp.sum(grad_v, axis=0, keepdims=True)
-    sums[0:1, :] = sum_u
-    sums[1:2, :] = sum_v
-    grad_far[...] = far_sum[...].astype(BF16)
-    for chip in range(2):
-        for side in range(2):
-            start = places[2 * chip + side]
-            pay[chip, side] = key_sum[rows_at(start), :].astype(BF16)
-            pay[chip, 2 + side] = key_sum[rows_at(start + LEN), :].astype(BF16)
-            pay[chip, 4 + side] = value_sum[rows_at(start), :].astype(BF16)
-            pay[chip, 6 + side] = value_sum[rows_at(start + LEN), :].astype(BF16)
-            pay[chip, 8 + side] = grad_query[rows_at(start), :]
-
-
-def attention_back(spot, own, peer, qu, qv, keys, values, far_rel, probs, attended):
-    return local_call(
-        attention_back_kernel,
-        [struct((2, 10, BLOCK, SLOT)), struct((2, SLOT), F32), struct((2 * LEN, SLOT))],
-        [pltpu.VMEM((LEN, SLOT), BF16)] * 2 + [pltpu.VMEM((2 * LEN, SLOT), F32)] * 3,
-        smem=1,
-        vmem=9,
-    )(spot, own, peer, qu, qv, keys, values, far_rel, probs, attended)
-
-
 def unproject_kernel(spot, own, peer, normed, experts, logits, route, grad_logit, wide, grad_part, grad_wide, grad_all, turned):
     step = pl.program_id(0)
     flat = [own[step], own[4 + step], peer[step], peer[4 + step]]
@@ -567,27 +493,6 @@
     )(spot, own, peer, normed, experts, logits, route, grad_logit, wide)
 
 
-def finish_kernel(rows, grad_mine, grad_theirs, gain, grad_resid, grad_tokens, sums):
-    gain_sum = jnp.zeros((1, D), F32)
-    bias_sum = jnp.zeros((1, D), F32)
-    for part in range(2):
-        here = slice(2 * part * BLOCK, (2 * part + 1) * BLOCK)
-        scaled, inverse = centered(rows[here, :].astype(F32))
-        grad = grad_mine[here, :].astype(F32) + grad_theirs[part].astype(F32)
-        gain_sum += jnp.sum(grad * scaled, axis=0, keepdims=True)
-        bias_sum += jnp.sum(grad, axis=0, keepdims=True)
-        if part == 1:
-            grad_tokens[...] = grad_resid[...] + norm_back(grad, scaled, inverse, gain[...].astype(F32))
-    sums[0:1, :] = gain_sum
-    sums[1:2, :] = bias_sum
-
-
-def finish(rows, grad_mine, grad_theirs, gain, grad_resid):
-    return local_call(finish_kernel, [struct((BLOCK, D), F32), struct((8, D), F32)], vmem=5)(
-        rows, grad_mine, grad_theirs, gain, grad_resid
-    )
-
-
 def place():
     dp = lax.axis_index("dp")
     sq = lax.axis_index("seq")
@@ -646,189 +551,451 @@
     lax.fori_loop(0, count, run, 0)
 
 
-def reduce_kernel(layouts, pieces, *refs):
-    count = len(layouts)
+class Links:
+    def __init__(self, send_sem, recv_sem):
+        self.send_sem, self.recv_sem, self.made = send_sem, recv_sem, []
+
+    def prepared(self, src, dst, device):
+        slot = len(self.made)
+        copy = pltpu.make_async_remote_copy(
+            src_ref=src,
+            dst_ref=dst,
+            send_sem=self.send_sem.at[slot],
+            recv_sem=self.recv_sem.at[slot],
+            device_id=device,
+            device_id_type=MESH,
+        )
+        self.made.append(copy)
+        return copy
+
+    def send(self, src, dst, device):
+        copy = self.prepared(src, dst, device)
+        copy.start()
+        return copy
+
+
+def added(target, *terms):
+    def add(index):
+        total = terms[0][index].astype(F32)
+        for term in terms[1:]:
+            total += term[index].astype(F32)
+        target[index] = total.astype(target.dtype)
+
+    return add
+
+
+class Stage:
+    def __init__(self, links, at, ref, dims, axis, width, bufs, after):
+        self.links, self.at, self.axis, self.bufs, self.after = links, at, axis, bufs, after
+        self.left = lead_shape(without(dims, axis))
+        self.cols = [pl.ds(*half) for half in halves(width)]
+        self.near = [chunk_of(ref, dims, axis, (at[axis] + steps) % 4) for steps in range(4)]
+        self.made = []
+
+    def launch_far(self):
+        for side, steps in ((0, 1), (1, 3)):
+            src = self.near[2].at[..., self.cols[side]]
+            self.made.append(self.links.send(src, self.bufs[side], moved(self.at, self.axis, steps)))
+
+    def launch_near(self):
+        for side, steps in ((0, 1), (1, 3)):
+            src = self.near[steps].at[..., self.cols[1 - side]]
+            self.made.append(self.links.send(src, self.bufs[2 + side], moved(self.at, self.axis, steps)))
+
+    def forward(self):
+        for side, steps in ((0, 1), (1, 3)):
+            self.made[side].wait_recv()
+            held = self.bufs[side]
+            each_block(self.left, added(held, held, self.near[steps].at[..., self.cols[side]]))
+            self.made.append(self.links.send(held, self.bufs[4 + side], moved(self.at, self.axis, steps)))
+
+    def collect(self):
+        for copy in self.made[2:]:
+            copy.wait_recv()
+        for side in (0, 1):
+            cols = self.cols[side]
+            terms = self.near[0].at[..., cols], self.bufs[4 + side], self.bufs[3 - side]
+            each_block(self.left, added(self.after.at[..., cols], *terms))
+
+
+def stage_scratch(dims, axis, rows, width):
+    left = lead_shape(without(dims, axis))
+    (_, one), (_, two) = halves(width)
+    return [pltpu.VMEM(left + (rows, size), BF16) for size in (one, two, two, one, one, two)]
+
+
+def launch(stages):
+    for stage in stages:
+        stage.launch_far()
+    for stage in stages:
+        stage.launch_near()
+
+
+def greet(devices):
+    barrier = pltpu.get_barrier_semaphore()
+    for device in devices:
+        pl.semaphore_signal(barrier, inc=1, device_id=device, device_id_type=MESH)
+
+
+UP, DOWN, OUT, WIDE_GRAD, REST = range(5)
+LAYOUTS = (PLAIN, SPLIT, PLAIN, PLAIN, PLAIN)
+SHAPES = ((16, FF // 2), (32, D), (16, EXPERTS), (16, WIDE), (16, 2 * SLOT))
+EARLY = (
+    (UP, 0, 1792, "xyz"),
+    (DOWN, 0, 768, "yzx"),
+    (OUT, 0, 256, "yzx"),
+    (OUT, 256, 1024, "zxy"),
+    (UP, 1792, 256, "zxy"),
+    (DOWN, 768, 256, "zxy"),
+)
+LATE = (
+    (WIDE_GRAD, 0, 768, "xyz"),
+    (WIDE_GRAD, 768, 768, "yzx"),
+    (WIDE_GRAD, 1536, 384, "zxy"),
+    (REST, 0, 256, "zxy"),
+)
+
+
+def dims_after(piece, phases):
+    return without(LAYOUTS[piece[0]], piece[3][:phases])
+
+
+def after_shape(piece, phases):
+    return lead_shape(dims_after(piece, phases)) + (SHAPES[piece[0]][0], piece[2])
+
+
+def phase_scratch(piece, phase):
+    return stage_scratch(dims_after(piece, phase), piece[3][phase], SHAPES[piece[0]][0], piece[2])
+
+
+def stage_for(links, at, piece, phase, ref, bufs, after):
+    return Stage(links, at, ref, dims_after(piece, phase), piece[3][phase], piece[2], bufs, after)
+
+
+KEY_BLOCKS = 2 * LEN // BLOCK
+
+
+def attention_back_kernel(*refs):
     refs = list(refs)
-    take = lambda number: [refs.pop(0) for _ in range(number)]
-    sources = take(count)
-    (small_in,) = take(1)
-    mine = take(count)
-    theirs = take(sum(dims is PLAIN for dims in layouts))
-    (small_out,) = take(1)
-    send_sem, recv_sem, own_sem = take(3)
-    totals = take(count)
-    small_slots = take(4)
+    take = lambda count: [refs.pop(0) for _ in range(count)]
+    given, qu, qv, keys, values, far_rel, probs, attended = take(8)
+    grads = take(3)
+    pay, pay_in, sums, grad_far = take(4)
+    afters = take(len(EARLY))
+    send_sem, recv_sem = take(2)
+    given_in, grad_out, grad_scores, grad_u, grad_query, grad_keys, grad_values, far_sum = take(8)
+    links = Links(send_sem, recv_sem)
     at = place()
+    peer = moved(at, "y", 2)
+    devices = [moved(at, axis, steps) for axis in "xyz" for steps in (1, 3)] + [peer]
+    greet(devices)
+    pl.semaphore_wait(pltpu.get_barrier_semaphore(), len(devices))
+    arrived = links.send(given.at[1], given_in, peer)
+    stages = []
+    for piece, after in zip(EARLY, afters):
+        source = grads[piece[0]].at[..., pl.ds(piece[1], piece[2])]
+        stages.append(stage_for(links, at, piece, 0, source, take(6), after))
+    launch(stages)
+    places = spots_of(at["core"], at["y"] // 2)
+    for side in range(2):
+        grad_out[rows_at(places[side]), :] = given[0, side]
+    arrived.wait_recv()
+    for side in range(2):
+        grad_out[rows_at(places[2 + side]), :] = given_in[side]
+    moving = []
+
+    def give(first, held, base):
+        for side in range(2):
+            pay[first + side] = held[rows_at(places[side] + base), :]
+            src = held.at[rows_at(places[2 + side] + base)]
+            moving.append(links.send(src, pay_in.at[first + side], peer))
+
+    def rows_seeing(block):
+        return pl.ds(max(0, block - 4) * BLOCK, LEN - max(0, block - 4) * BLOCK)
+
+    for block in range(KEY_BLOCKS):
+        cols, rows = pl.ds(block * BLOCK, BLOCK), rows_seeing(block)
+        grad_values[cols, :] = dot(probs[rows, cols], grad_out[rows, :], 0, 0).astype(BF16)
+    give(4, grad_values, 0)
+    give(6, grad_values, LEN)
+    blocks = LEN // BLOCK
+    sum_u = jnp.zeros((1, SLOT), F32)
+    for block in range(blocks):
+        rows = pl.ds(block * BLOCK, BLOCK)
+        width = LEN + (block + 1) * BLOCK
+        above = grad_out[rows, :]
+        grad_probs = dot(above, values[:width, :], 1, 1)
+        inner = jnp.sum(above.astype(F32) * attended[rows, :], axis=1, keepdims=True)
+        scores = (probs[rows, :width].astype(F32) * ((grad_probs - inner) * SCALE)).astype(BF16)
+        grad_scores[rows, :width] = scores
+        part = dot(scores, keys[:width, :])
+        grad_u[rows, :] = part
+        sum_u += jnp.sum(part, axis=0, keepdims=True)
+    for stage in stages:
+        stage.forward()
+    for block in range(KEY_BLOCKS):
+        cols, rows = pl.ds(block * BLOCK, BLOCK), rows_seeing(block)
+        grad_keys[cols, :] = dot(grad_scores[rows, cols], qu[rows, :], 0, 0).astype(BF16)
+    give(0, grad_keys, 0)
+    give(2, grad_keys, LEN)
+    far_sum[...] = jnp.zeros_like(far_sum)
+    down = lax.broadcasted_iota(jnp.int32, (BLOCK, BLOCK), 0)
+    across = lax.broadcasted_iota(jnp.int32, (BLOCK, BLOCK), 1)
+    flip = (down + across == BLOCK - 1).astype(F32).astype(BF16)
+    sum_v = jnp.zeros((1, SLOT), F32)
+    for block in range(blocks):
+        rows = pl.ds(block * BLOCK, BLOCK)
+        width = LEN + (block + 1) * BLOCK
+        first_far = 2 * LEN - width
+        far = pltpu.roll(dot(flip, grad_scores[rows, :width]), 0, 1, stride=1, stride_axis=0).astype(BF16)
+        turned = dot(flip, far).astype(BF16)
+        part = dot(turned, far_rel[first_far:, :])
+        far_sum[first_far:, :] += dot(turned, qv[rows, :], 0, 0)
+        grad_query[rows, :] = (grad_u[rows, :] + part).astype(BF16)
+        sum_v += jnp.sum(part, axis=0, keepdims=True)
+    give(8, grad_query, 0)
+    sums[0:1, :] = sum_u
+    sums[1:2, :] = sum_v
+    grad_far[...] = far_sum[...].astype(BF16)
+    for stage in stages:
+        stage.collect()
+    for copy in moving:
+        copy.wait_recv()
+    for copy in links.made:
+        copy.wait_send()
+
+
+def attention_back(given, qu, qv, keys, values, far_rel, probs, attended, grads):
+    scratch = []
+    for piece in EARLY:
+        scratch += phase_scratch(piece, 0)
+    copies = 1 + 10 + 6 * len(EARLY)
+    seq = (2 * LEN, SLOT)
+    outs = [struct((10, BLOCK, SLOT)), struct((10, BLOCK, SLOT)), struct((2, SLOT), F32), struct(seq)]
+    outs += [struct(after_shape(piece, 1)) for piece in EARLY]
+    return pl.pallas_call(
+        attention_back_kernel,
+        out_shape=outs,
+        in_specs=[IN_VMEM] * 11,
+        out_specs=[IN_VMEM] * len(outs),
+        scratch_shapes=[
+            pltpu.SemaphoreType.DMA((copies,)),
+            pltpu.SemaphoreType.DMA((copies,)),
+            pltpu.VMEM((2, BLOCK, SLOT), BF16),
+            pltpu.VMEM((LEN, SLOT), BF16),
+            pltpu.VMEM((LEN, 2 * LEN), BF16),
+            pltpu.VMEM((LEN, SLOT), F32),
+            pltpu.VMEM((LEN, SLOT), BF16),
+            pltpu.VMEM(seq, BF16),
+            pltpu.VMEM(seq, BF16),
+            pltpu.VMEM(seq, F32),
+        ]
+        + scratch,
+        compiler_params=pltpu.CompilerParams(
+            collective_id=1, has_side_effects=True, vmem_limit_bytes=VMEM_BYTES
+        ),
+    )(given, qu, qv, keys, values, far_rel, probs, attended, *grads)
+
+
+COUNT_ROW = 2 * H
+VECTOR_ROW = 16
+UP_BIAS_ROW = VECTOR_ROW + 5 * 8
+SMALL_ROWS = UP_BIAS_ROW + FF // SLOT
+
+
+def lay(target, first, vector):
+    for row in range(vector.shape[1] // SLOT):
+        target[first + row : first + row + 1, :] = vector[:, row * SLOT : (row + 1) * SLOT]
+
+
+def final_kernel(*refs):
+    refs = list(refs)
+    take = lambda count: [refs.pop(0) for _ in range(count)]
+    rows, part, gain, grad_resid, feed_sums, grad_up_bias, small_in = take(7)
+    early = take(len(EARLY))
+    late = dict(zip((WIDE_GRAD, REST), take(2)))
+    grad_tokens, small_out, down_out = take(3)
+    both = dict(zip((UP, OUT, WIDE_GRAD, REST), take(4)))
+    send_sem, recv_sem, own_sem, part_in, half_bias = take(5)
+    totals = take(5)
+    slots = take(4)
+    links = Links(send_sem, recv_sem)
+    at = place()
+    core = at["core"]
     sibling = dict(at)
-    sibling["core"] = 1 - at["core"]
+    sibling["core"] = 1 - core
     sibling = device_of(sibling)
-    high, low, core = at["x"] // 2, at["x"] % 2, at["core"]
+    high, low = at["x"] // 2, at["x"] % 2
     stays = (high == low) & (low == core)
     ahead, behind = dict(at), dict(at)
     ahead["x"], ahead["core"] = 2 * core + high, low
     behind["x"], behind["core"] = 2 * low + core, high
     ahead, behind = device_of(ahead), device_of(behind)
-    barrier = pltpu.get_barrier_semaphore()
-    greeted = [moved(at, axis, steps) for axis in "xyz" for steps in (1, 2, 3)] + [sibling]
-
-    def greet(device):
-        pl.semaphore_signal(barrier, inc=1, device_id=device, device_id_type=pl.DeviceIdType.MESH)
-
-    for device in greeted:
-        greet(device)
-
-    def greet_far():
-        greet(ahead)
-        greet(behind)
-        pl.semaphore_wait(barrier, len(greeted) + 2)
-
-    pl.when(jnp.logical_not(stays))(greet_far)
-    pl.when(stays)(lambda: pl.semaphore_wait(barrier, len(greeted)))
-    used = [0]
-
-    def prepared(src, dst, device):
-        slot = used[0]
-        used[0] += 1
-        return pltpu.make_async_remote_copy(
-            src_ref=src,
-            dst_ref=dst,
-            send_sem=send_sem.at[slot],
-            recv_sem=recv_sem.at[slot],
-            device_id=device,
-            device_id_type=pl.DeviceIdType.MESH,
-        )
-
-    def send(src, dst, device):
-        copy = prepared(src, dst, device)
-        copy.start()
-        return copy
-
-    def added(target, *terms):
-        def add(index):
-            total = terms[0][index].astype(F32)
-            for term in terms[1:]:
-                total += term[index].astype(F32)
-            target[index] = total.astype(target.dtype)
-
-        return add
-
-    current = [sources[array].at[..., pl.ds(start, width)] for array, start, width, order in pieces]
-    small_now = small_in
-    open_sends = []
-    for phase in range(3):
-        plans = []
-        for number, (array, start, width, order) in enumerate(pieces):
-            axis = order[phase]
-            dims = without(layouts[array], order[:phase])
-            left = lead_shape(without(dims, axis))
-            cols = [pl.ds(*half) for half in halves(width)]
+    devices = [moved(at, axis, steps) for axis in "xyz" for steps in (1, 2, 3)] + [sibling]
+    greet(devices)
+
+    def greet_more():
+        greet([ahead, behind])
+        pl.semaphore_wait(pltpu.get_barrier_semaphore(), len(devices) + 2)
+
+    pl.when(jnp.logical_not(stays))(greet_more)
+    pl.when(stays)(lambda: pl.semaphore_wait(pltpu.get_barrier_semaphore(), len(devices)))
+    halves_in = [links.send(part.at[2 * side + 1], part_in.at[side], sibling) for side in range(2)]
+
+    jobs = []
+    for piece in LATE:
+        jobs.append([piece, 0, late[piece[0]].at[..., pl.ds(piece[1], piece[2])]])
+    for piece, ref in zip(EARLY, early):
+        jobs.append([piece, 1, ref])
+
+    def begin():
+        stages = []
+        for job in jobs:
+            piece, phase, ref = job
             bufs = take(6)
-            after = take(1)[0] if phase < 2 else totals[array].at[:, pl.ds(start, width)]
-            near = [chunk_of(current[number], dims, axis, (at[axis] + steps) % 4) for steps in range(4)]
-            plans.append((axis, left, cols, bufs, after, near, []))
-        for axis, left, cols, bufs, after, near, made in plans:
-            for side, steps in ((0, 1), (1, 3)):
-                made.append(send(near[2].at[..., cols[side]], bufs[side], moved(at, axis, steps)))
-        small_axis = "xyz"[phase]
-        slots = small_slots[phase]
-        small_copies = []
-        slots[at[small_axis]] = small_now[...]
-        for steps in (1, 2, 3):
-            small_copies.append(
-                send(slots.at[at[small_axis]], slots.at[at[small_axis]], moved(at, small_axis, steps))
-            )
-        for axis, left, cols, bufs, after, near, made in plans:
-            for side, steps in ((0, 1), (1, 3)):
-                made.append(
-                    send(near[steps].at[..., cols[1 - side]], bufs[2 + side], moved(at, axis, steps))
-                )
-        for axis, left, cols, bufs, after, near, made in plans:
-            for side, steps in ((0, 1), (1, 3)):
-                made[side].wait_recv()
-                each_block(left, added(bufs[side], bufs[side], near[steps].at[..., cols[side]]))
-                made.append(send(bufs[side], bufs[4 + side], moved(at, axis, steps)))
-        for copy in small_copies:
+            after = take(1)[0] if phase < 2 else totals[piece[0]].at[:, pl.ds(piece[1], piece[2])]
+            stages.append(stage_for(links, at, piece, phase, ref, bufs, after))
+            job[1:] = [phase + 1, after]
+        launch(stages)
+        jobs[:] = [job for job in jobs if job[1] < 3]
+        return stages
+
+    def spread(number, value):
+        axis = "xyz"[number]
+        here = slots[number].at[at[axis]]
+        here[...] = value
+        return [links.send(here, here, moved(at, axis, steps)) for steps in (1, 2, 3)]
+
+    def gathered(number, copies):
+        for copy in copies:
             copy.wait_recv()
-        small_total = (slots[0] + slots[1]) + (slots[2] + slots[3])
-        small_now = small_slots[3].at[core] if phase == 2 else small_out
-        small_now[...] = small_total
-        open_sends += small_copies
-        current = []
-        for axis, left, cols, bufs, after, near, made in plans:
-            for copy in made[2:]:
-                copy.wait_recv()
-            for side in (0, 1):
-                each_block(
-                    left,
-                    added(
-                        after.at[..., cols[side]],
-                        near[0].at[..., cols[side]],
-                        bufs[4 + side],
-                        bufs[3 - side],
-                    ),
-                )
-            open_sends += made
-            current.append(after)
+        one = slots[number]
+        return (one[0] + one[1]) + (one[2] + one[3])
+
+    stages = begin()
+    for copy in halves_in:
+        copy.wait_recv()
+    gain_sum = jnp.zeros((1, D), F32)
+    bias_sum = jnp.zeros((1, D), F32)
+    for side in range(2):
+        scaled, inverse = centered(rows[side].astype(F32))
+        grad = part[2 * side].astype(F32) + part_in[side].astype(F32)
+        gain_sum += jnp.sum(grad * scaled, axis=0, keepdims=True)
+        bias_sum += jnp.sum(grad, axis=0, keepdims=True)
+        if side == 1:
+            grad_tokens[...] = grad_resid[...] + norm_back(grad, scaled, inverse, gain[...].astype(F32))
+    small = small_out
+    small[:VECTOR_ROW, :] = small_in[...]
+    lay(small, VECTOR_ROW, gain_sum)
+    lay(small, VECTOR_ROW + 8, bias_sum)
+    for number in range(3):
+        lay(small, VECTOR_ROW + 16 + 8 * number, feed_sums[number : number + 1, :])
+    small[UP_BIAS_ROW:, :] = jnp.zeros((FF // SLOT, SLOT), F32)
+    lay(half_bias, 0, grad_up_bias[...])
+    half = FF // 2 // SLOT
+    small[pl.ds(pl.multiple_of(UP_BIAS_ROW + core * half, 8), half), :] = half_bias[...]
+    copies = spread(0, small[...])
+    for stage in stages:
+        stage.forward()
+    for stage in stages:
+        stage.collect()
+    stages = begin()
+    copies = spread(1, gathered(0, copies))
+    for stage in stages:
+        stage.forward()
+    for stage in stages:
+        stage.collect()
+    stages = begin()
+    copies = spread(2, gathered(1, copies))
+    for stage in stages:
+        stage.forward()
+    for stage in stages:
+        stage.collect()
     last = []
-    pair = small_slots[3]
-    last.append(send(pair.at[core], pair.at[core], sibling))
-    spare = list(theirs)
-    for array, dims in enumerate(layouts):
-        if dims is PLAIN:
-            half = totals[array].shape[0] // 2
-            other = pl.ds(pl.multiple_of((1 - core) * half, 8), half)
-            last.append(send(totals[array].at[other], spare.pop(0), sibling))
-            mine[array][...] = totals[array][pl.ds(pl.multiple_of(core * half, 8), half), :]
-            continue
-        away = prepared(totals[array], mine[array], ahead)
-        here = pltpu.make_async_copy(totals[array], mine[array], own_sem)
-        pl.when(jnp.logical_not(stays))(away.start)
-        pl.when(stays)(here.start)
-        pl.when(jnp.logical_not(stays))(away.wait)
-        pl.when(stays)(here.wait)
+    pair = slots[3]
+    pair[core] = gathered(2, copies)
+    last.append(links.send(pair.at[core], pair.at[core], sibling))
+    away = links.prepared(totals[DOWN], down_out, ahead)
+    here = pltpu.make_async_copy(totals[DOWN], down_out, own_sem)
+    pl.when(jnp.logical_not(stays))(away.start)
+    pl.when(stays)(here.start)
+    for array, out in both.items():
+        other = pl.ds(pl.multiple_of((1 - core) * 8, 8), 8)
+        last.append(links.send(totals[array].at[other], out.at[core], sibling))
+        out[core] = totals[array][pl.ds(pl.multiple_of(core * 8, 8), 8), :]
     for copy in last:
         copy.wait_recv()
     small_out[...] = pair[0] + pair[1]
-    for copy in open_sends + last:
-        copy.wait_send()
-
-
-def reduce_all(arrays, layouts, pieces, small):
-    shapes = [array.shape[1:] for array in arrays]
-    arrays = [
-        array.reshape(lead_shape(dims) + shape) for array, dims, shape in zip(arrays, layouts, shapes)
-    ]
+    pl.when(jnp.logical_not(stays))(away.wait)
+    pl.when(stays)(here.wait)
+    for copy in links.made:
+        if copy is not away:
+            copy.wait_send()
+
+
+def final(rows, part, gain, grad_resid, feed_sums, grad_up_bias, small, early, late):
+    jobs = [(piece, 0) for piece in LATE] + [(piece, 1) for piece in EARLY]
     scratch = []
-    copies = 0
-    for phase in range(3):
-        for array, start, width, order in pieces:
-            left = lead_shape(without(layouts[array], order[: phase + 1]))
-            rows = shapes[array][0]
-            (_, one), (_, two) = halves(width)
-            for size in (one, two, two, one, one, two):
-                scratch.append(pltpu.VMEM(left + (rows, size), BF16))
+    copies = 2 + 9 + 1 + 1 + 4
+    while jobs:
+        for piece, phase in jobs:
+            scratch += phase_scratch(piece, phase)
+            copies += 6
             if phase < 2:
-                scratch.append(pltpu.VMEM(left + (rows, width), BF16))
-            copies += 6
-    copies += 9 + len(arrays) + 1
-    head = [pltpu.SemaphoreType.DMA((copies,)), pltpu.SemaphoreType.DMA((copies,)), pltpu.SemaphoreType.DMA]
-    head += [pltpu.VMEM(shape, F32) for shape in shapes]
-    head += [pltpu.VMEM((4,) + small.shape, F32)] * 3 + [pltpu.VMEM((2,) + small.shape, F32)]
-    outs = []
-    for shape, dims in zip(shapes, layouts):
-        outs.append(struct((shape[0] // 2 if dims is PLAIN else shape[0], shape[1]), F32))
-    outs += [out for out, dims in zip(outs, layouts) if dims is PLAIN]
-    outs.append(struct(small.shape, F32))
+                scratch.append(pltpu.VMEM(after_shape(piece, phase + 1), BF16))
+        jobs = [(piece, phase + 1) for piece, phase in jobs if phase < 2]
+    outs = [struct((BLOCK, D), F32), struct((SMALL_ROWS, SLOT), F32), struct(SHAPES[DOWN], F32)]
+    outs += [struct((2, 8, SHAPES[array][1]), F32) for array in (UP, OUT, WIDE_GRAD, REST)]
     return pl.pallas_call(
-        partial(reduce_kernel, layouts, pieces),
+        final_kernel,
         out_shape=outs,
-        in_specs=[IN_VMEM] * (len(arrays) + 1),
+        in_specs=[IN_VMEM] * (7 + len(EARLY) + 2),
         out_specs=[IN_VMEM] * len(outs),
-        scratch_shapes=head + scratch,
+        scratch_shapes=[
+            pltpu.SemaphoreType.DMA((copies,)),
+            pltpu.SemaphoreType.DMA((copies,)),
+            pltpu.SemaphoreType.DMA,
+            pltpu.VMEM((2, BLOCK, D), BF16),
+            pltpu.VMEM((FF // 2 // SLOT, SLOT), F32),
+        ]
+        + [pltpu.VMEM(shape, F32) for shape in SHAPES]
+        + [pltpu.VMEM((4, SMALL_ROWS, SLOT), F32)] * 3
+        + [pltpu.VMEM((2, SMALL_ROWS, SLOT), F32)]
+        + scratch,
         compiler_params=pltpu.CompilerParams(
-            collective_id=0, has_side_effects=True, vmem_limit_bytes=VMEM_BYTES
+            collective_id=2, has_side_effects=True, vmem_limit_bytes=VMEM_BYTES
         ),
-    )(*arrays, small)
+    )(rows, part, gain, grad_resid, feed_sums, grad_up_bias, small, *early, *late)
+
+
+def arrange_kernel(up, out, wide, rest, grad_up, grad_out, grad_value, grad_key, grad_query, grad_rel, grad_routers):
+    grad_up[:, : FF // 2] = up[0]
+    grad_up[:, FF // 2 :] = up[1]
+    for head in range(H):
+        core, pair = head % 2, head // 2
+        for expert in range(E):
+            slot = (pair * E + expert) * SLOT
+            start = (head * E + expert) * DH
+            grad_out[:, start : start + DH] = out[core, :, slot : slot + DH]
+            grad_value[:, start : start + DH] = wide[core, :, slot : slot + DH]
+        start = head * DH
+        for target, source, slot in (
+            (grad_key, wide, KEY_AT),
+            (grad_query, wide, QUERY_AT),
+            (grad_rel, rest, 0),
+        ):
+            slot += pair * SLOT
+            target[:, start : start + DH] = source[core, :, slot : slot + DH]
+    for kind in range(2):
+        for head in range(H):
+            at = ROUTER_AT + (2 * kind + head // 2) * E
+            start = (kind * H + head) * E
+            grad_routers[:, start : start + E] = wide[head % 2, :, at : at + E]
+
+
+def arrange(up, out, wide, rest):
+    widths = (FF, H * E * DH, H * E * DH, H * DH, H * DH, H * DH, 2 * H * E)
+    return local_call(arrange_kernel, [struct((8, width), F32) for width in widths], vmem=4)(up, out, wide, rest)
 
 
 def sinus_far():
@@ -936,26 +1103,27 @@
         final_mine,
         swap(final_theirs),
     )
-    pay_back, bias_sums, grad_far = attention_back(
-        spot, grad_att[0], cross(grad_att[1]), qu, qv, keys, values, far_rel, probs, attended
+    pay_back, pay_in, bias_sums, grad_far, *early = attention_back(
+        grad_att,
+        qu,
+        qv,
+        keys,
+        values,
+        far_rel,
+        probs,
+        attended,
+        [
+            grad_up.reshape(lead_shape(PLAIN) + SHAPES[UP]),
+            grad_down.reshape(lead_shape(SPLIT) + SHAPES[DOWN]),
+            grad_out.reshape(lead_shape(PLAIN) + SHAPES[OUT]),
+        ],
     )
     grad_rel = dot(sinus, grad_far, 0, 0).astype(BF16)
     part, grad_wide = unproject(
-        spot, pay_back[0], cross(pay_back[1]), normed, experts, logits, value_routes, grad_out_logit, wide
-    )
-    part_theirs = swap(part.reshape(2, 2, BLOCK, D)[:, 1])
-    grad_tokens, attn_sums = finish(rows, part, part_theirs, attn_gain, grad_resid)
-    nothing = jnp.zeros((), F32)
-    up_bias_full = jnp.concatenate(
-        [jnp.where(core == 0, grad_up_bias[0], nothing), jnp.where(core == 1, grad_up_bias[0], nothing)]
-    )
-    narrow = jnp.concatenate(
-        [attn_sums[:2].T, feed_sums[:3].T, up_bias_full.reshape(D, 4), jnp.zeros((D, SLOT - 9), F32)], axis=1
-    ).astype(BF16)
+        spot, pay_back, pay_in, normed, experts, logits, value_routes, grad_out_logit, wide
+    )
     blank = jnp.zeros((), BF16)
-    rest = jnp.concatenate(
-        [jnp.where(chip == 0, grad_rel, blank), jnp.where(chip == 1, grad_rel, blank), narrow], axis=1
-    )
+    rest = jnp.concatenate([jnp.where(chip == 0, grad_rel, blank), jnp.where(chip == 1, grad_rel, blank)], axis=1)
     picks = jnp.arange(E, dtype=jnp.int32)
     chosen = (routes.reshape(3 * BLOCK, H, 2)[..., None] == picks).astype(F32).sum(axis=2)
     counts = jnp.concatenate(
@@ -967,70 +1135,52 @@
             head_at * bias_sums[0:1],
             head_at * bias_sums[1:2],
             jnp.pad(counts, (0, SLOT - 40)).reshape(1, SLOT),
-            jnp.zeros((7, SLOT), F32),
+            jnp.zeros((VECTOR_ROW - COUNT_ROW - 1, SLOT), F32),
         ],
         axis=0,
     )
-    pieces = (
-        (0, 0, 2048, "xyz"),
-        (1, 0, 1024, "yzx"),
-        (2, 0, 1408, "zxy"),
-        (3, 0, 768, "zxy"),
-        (4, 0, 384, "zxy"),
-        (2, 1408, 512, "xyz"),
-        (3, 768, 512, "yzx"),
-    )
-    layouts = (PLAIN, SPLIT, PLAIN, PLAIN, PLAIN)
-    up_mine, down_mine, wide_mine, out_mine, rest_mine, up_their, wide_their, out_their, rest_their, small_sum = (
-        reduce_all(
-            [
-                grad_up.reshape(64, 16, FF // 2),
-                grad_down.reshape(64, 32, D),
-                grad_wide.reshape(64, 16, WIDE),
-                grad_out.reshape(64, 16, EXPERTS),
-                rest.reshape(64, 16, 3 * SLOT),
-            ],
-            layouts,
-            pieces,
-            small,
-        )
-    )
-    first = core == 0
-
-    def cores(mine, theirs):
-        return jnp.stack([jnp.where(first, mine, theirs), jnp.where(first, theirs, mine)])
-
-    def by_head(both, parts, width):
-        shaped = both.reshape(2, 8, 2, parts, -1)[..., :width]
-        return shaped.transpose(1, 2, 0, 3, 4).reshape(8, H * parts * width)
-
-    wide_both = cores(wide_mine, wide_their)
-    out_both = cores(out_mine, out_their)
-    rest_both = cores(rest_mine, rest_their)
-    narrow_sum = rest_mine[:, 2 * SLOT :] + rest_their[:, 2 * SLOT :]
-    up_both = cores(up_mine, up_their)
+    grad_tokens, small_sum, grad_down_own, up_both, out_both, wide_both, rest_both = final(
+        jnp.stack([memory, tokens]),
+        part.reshape(4, BLOCK, D),
+        attn_gain,
+        grad_resid,
+        feed_sums,
+        grad_up_bias,
+        small,
+        early,
+        [
+            grad_wide.reshape(lead_shape(PLAIN) + SHAPES[WIDE_GRAD]),
+            rest.reshape(lead_shape(PLAIN) + SHAPES[REST]),
+        ],
+    )
+    grad_up_own, grad_out_own, grad_value, grad_key, grad_query, grad_relative, grad_routers = arrange(
+        up_both, out_both, wide_both, rest_both
+    )
+    device = lax.axis_index("dp") * 4 + seq_index
+    vectors = lax.dynamic_slice_in_dim(small_sum[VECTOR_ROW:UP_BIAS_ROW].reshape(5, D), device * 8, 8, 1)
+    grad_up_bias_own = lax.dynamic_slice_in_dim(small_sum[UP_BIAS_ROW:].reshape(FF), device * 32, 32, 0)
     per_head = lambda rows: rows[:, :DH].reshape(H * DH)
     return (
         result[None],
         grad_tokens[None],
-        narrow_sum[:, 0],
-        narrow_sum[:, 1],
-        by_head(wide_both[..., QUERY_AT:ROUTER_AT], 1, DH),
-        by_head(wide_both[..., KEY_AT:QUERY_AT], 1, DH),
-        by_head(rest_both[..., : 2 * SLOT], 1, DH),
-        per_head(small_sum[:4]),
-        per_head(small_sum[4:8]),
-        by_head(wide_both[..., ROUTER_AT : ROUTER_AT + 10], E, 1),
-        by_head(wide_both[..., :EXPERTS], E, DH),
-        by_head(wide_both[..., ROUTER_AT + 10 : ROUTER_AT + 20], E, 1),
-        by_head(out_both, E, DH).T,
-        narrow_sum[:, 2],
-        narrow_sum[:, 3],
-        jnp.concatenate([up_both[0], up_both[1]], axis=1),
-        narrow_sum[:, 5:9].reshape(-1),
-        down_mine,
-        narrow_sum[:, 4],
-        jnp.round(small_sum[8, :40]).astype(jnp.int32).reshape(2, H, E),
+        vectors[0],
+        vectors[1],
+        grad_query,
+        grad_key,
+        grad_relative,
+        per_head(small_sum[:H]),
+        per_head(small_sum[H : 2 * H]),
+        grad_routers[:, : H * E],
+        grad_value,
+        grad_routers[:, H * E :],
+        grad_out_own.T,
+        vectors[2],
+        vectors[3],
+        grad_up_own,
+        grad_up_bias_own,
+        grad_down_own,
+        vectors[4],
+        jnp.round(small_sum[COUNT_ROW, :40]).astype(jnp.int32).reshape(2, H, E),
     )
 
 

time: 327 us -> 302 us (0.924)
  waiting for transfers between devices: 32.1 us -> 15.1 us
  Pallas kernels: 212 us -> 226 us
  local copies, waits for them, and re-layouts: 39.1 us -> 27.3 us
  starting transfers between devices: 18.2 us -> 10.3 us
    ppermute x4 -> x2, waiting for transfers between devices: 28.5 us -> 13.1 us  [cross(): return lax.ppermute(value, 'seq', [(0, 2), (2, 0), (1, 3), (3, 1)])]
    pallas_call x3, Pallas kernels: 109 us -> 123 us  [the longest x1 62.9 us: attention_back(): pl.pallas_call(attention_back_kernel, out_shape=outs, in_specs=[IN_VMEM]...]
    ppermute x4 -> x2, starting transfers between devices: 12.2 us -> 6.41 us  [cross(): return lax.ppermute(value, 'seq', [(0, 2), (2, 0), (1, 3), (3, 1)])]
    reshape x8 -> x2, local copies, waits for them, and re-layouts: 5.51 us -> 0.72 us  [the longest x1 0.72 us: body(): small_sum[UP_BIAS_ROW:].reshape(FF)]
    squeeze x3 -> x1, local copies, waits for them, and re-layouts: 5.17 us -> 0.53 us  [body(): vectors[4]]
    unnamed x50 -> x38, local copies, waits for them, and re-layouts: 8.4 us -> 7.75 us
  transfers between devices with their start and end apart: 12 -> 9, of which waited for: 6 -> 4; matrix products, arithmetic and copies ran while one was open for 7% -> 7% of each run, Pallas kernels for 2% -> 3%
where the time goes in v2:
time: 302 us; the launch traced here: 297 us
  Pallas kernels  226 us (75%)
  local copies, waits for them, and re-layouts  27.3 us (9%)
  waiting for transfers between devices  15.1 us (5%)
  other arithmetic  12.3 us (4%)
  starting transfers between devices  10.3 us (3%)
  matrix products  3.87 us (1%)
    pallas_call x1, Pallas kernels, attention_back(): pl.pallas_call(attention_back_kernel, out_shape=outs, in_specs=[IN_VMEM]...  62.9 us
    pallas_call x1, Pallas kernels, final(): pl.pallas_call(final_kernel, out_shape=outs, in_specs=[IN_VMEM] * (7 + le...  58.8 us
    pallas_call x1, Pallas kernels, unproject(): pl.pallas_call(unproject_kernel, grid=(4,), out_shape=[struct((4 * BLOCK,...  28.4 us
    pallas_call x1, Pallas kernels, feed(): pl.pallas_call(feed_kernel, grid_spec=pltpu.PrefetchScalarGridSpec(num_sc...  24 us
    pallas_call x1, Pallas kernels, project(): pl.pallas_call(project_kernel, grid=(4,), out_shape=[struct((4 * BLOCK, D...  13.5 us
    pallas_call x1, Pallas kernels, unmix(): local_call(unmix_kernel, [struct((BLOCK, D), F32), struct((2, 2, BLOCK, S...  13.3 us
    ppermute x2, waiting for transfers between devices, cross(): return lax.ppermute(value, 'seq', [(0, 2), (2, 0), (1, 3), (3, 1)])  13.1 us
    pallas_call x1, Pallas kernels, attention(): local_call(attention_kernel, [struct((LEN, SLOT), F32), struct((LEN, 2 *...  9.14 us
  transfers between devices with their start and end apart: 9, of which 4 were waited for; matrix products, arithmetic and copies ran while one was open for 7% of the time, Pallas kernels for 3%

profile of v2, /device:TPU:3, one launch (start us, length us, event | category | flops | bytes accessed | tf_op | source)
XLA Modules:
  0.0 297.0 jit_solution(17488817834580890817)
XLA Ops:
  8.5 1.3 reshape.262.gain.refs_2_
  9.8 1.3 reshape.263.shift
  11.0 7.7 %shard_map.374 = (bf16[1920,1024]{1,0:T(8,128)(2,1)}, bf16[128,1024]{1,0:T(8,128)(2,1)}, bf16[1280,1024]{1,0:T(8,128)(2,1)}) custom-call(s32[3]{0:T(128)} %pad_add_fusion.4.spot, bf16[2240,1024]{1,0:T(8,128)(2,1)} %bitcast.69, bf16[448,1024]{1,0:T(8,128)(2,1)} %bitcast.85, bf16[448,1024]{1,0:T(8,128)(2,1)} %bitcast.86, bf16[448,1024]{1,0:T(8,128)(2,1)} %bitcast.87, ...), custom_call_target="tpu_custom_call" | custom-call | tf_op jit(solution)/shard_map/pallas_call | solution.py:112
  19.5 0.9 pad_add_fusion
  20.4 1.5 pad_maximum_fusion.5.rows
  21.9 13.5 %shard_map.375 = (bf16[1024,1024]{1,0:T(8,128)(2,1)}, bf16[1024,1280]{1,0:T(8,128)(2,1)}, f32[1024,128]{1,0:T(8,128)}, bf16[2,10,256,128]{3,2,1,0:T(8,128)(2,1)}) custom-call(s32[3]{0:T(128)} %pad_add_fusion.4.spot, bf16[1024,1024]{1,0:T(8,128)(2,1)} %pad_maximum_fusion.5.rows, bf16[1,1024]{1,0:T(2,128)(2,1)} %reshape.262.gain.refs_2_, ...), custom_call_target="tpu_custom_call" | custom-call | tf_op jit(solution)/shard_map/pallas_call | solution.py:146
  35.4 2.3 select_bitcast_fusion
  37.6 3.4 %collective-permute-start.3 = (bf16[10,256,128]{2,1,0:T(8,128)(2,1)S(1)}, bf16[10,256,128]{2,1,0:T(8,128)(2,1)S(1)}, u32[]{:S(2)}, u32[]{:S(2)}) collective-permute-start(bf16[10,256,128]{2,1,0:T(8,128)(2,1)S(1)} %get-tuple-element.130), channel_id=1, source_target_pairs={{0,2},{2,0},{1,3},{3,1},{4,6},{6,4},{5,7},{7,5},{8,10},{10,8},{9,1... | collective-permute-start | bytes 1966088 | tf_op jit(solution)/shard_map/ppermute | solution.py:1017
  41.0 1.3 add_convert_fusion
  42.4 2.1 fusion.2.far_rel.refs_5_
  44.5 11.3 %collective-permute-done.3.peer = bf16[10,256,128]{2,1,0:T(8,128)(2,1)S(1)} collective-permute-done((bf16[10,256,128]{2,1,0:T(8,128)(2,1)S(1)}, bf16[10,256,128]{2,1,0:T(8,128)(2,1)S(1)}, u32[]{:S(2)}, u32[]{:S(2)}) %collective-permute-start.3) | collective-permute-done | bytes 655392 | tf_op jit(solution)/shard_map/ppermute | solution.py:1017
  56.6 9.1 %shard_map.376 = (f32[1024,128]{1,0:T(8,128)}, bf16[1024,2048]{1,0:T(8,128)(2,1)}, bf16[2048,128]{1,0:T(8,128)(2,1)}, bf16[2048,128]{1,0:T(8,128)(2,1)}, bf16[10...) custom-call(s32[3]{0:T(128)} %pad_add_fusion.4.spot, ...), custom_call_target="tpu_custom_call" | custom-call | tf_op jit(solution)/shard_map/pallas_call | solution.py:205
  65.8 1.6 fusion.8
  67.4 3.0 %collective-permute-start.4 = (bf16[2,256,128]{2,1,0:T(8,128)(2,1)S(1)}, bf16[2,256,128]{2,1,0:T(8,128)(2,1)S(1)}, u32[]{:S(2)}, u32[]{:S(2)}) collective-permute-start(bf16[2,256,128]{2,1,0:T(8,128)(2,1)S(1)} %get-tuple-element.136), channel_id=1, source_target_pairs={{0,2},{2,0},{1,3},{3,1},{4,6},{6,4},{5,7},{7,5},{8,10},{10,8},{9,1... | collective-permute-start | bytes 393224 | tf_op jit(solution)/shard_map/ppermute | solution.py:1017
  71.3 1.8 collective-permute-done.4.peer
  73.8 6.6 %shard_map.377 = (bf16[512,1280]{1,0:T(8,128)(2,1)}, bf16[512,1024]{1,0:T(8,128)(2,1)}) custom-call(s32[3]{0:T(128)} %pad_add_fusion.4.spot, bf16[2,256,128]{2,1,0:T(8,128)(2,1)} %get-tuple-element.137.own, bf16[2,256,128]{2,1,0:T(8,128)(2,1)} %copy-done.6, f32[1024,128]{1,0:T(8,128)} %get-tuple-element.79.logits, s32[512,8]{1,0:T(8,128)} %copy.71.route, ...), custom_call_target="tpu_custom_call" | custom-call | tf_op jit(solution)/shard_map/pallas_call | solution.py:240
  80.4 1.8 collective-permute-start.5
  85.4 2.1 pad_maximum_fusion.8.cot
  87.5 1.0 copy-done.4
  88.5 24.0 %shard_map.378 = (f32[512,1024]{1,0:T(8,128)}, f32[256,1024]{1,0:T(8,128)}, bf16[256,1024]{1,0:T(8,128)(2,1)}, bf16[512,1024]{1,0:T(8,128)(2,1)}, bf16[1024,2048...) custom-call(s32[3]{0:T(128)} %pad_add_fusion.4.spot, bf16[1024,1024]{1,0:T(8,128)(2,1)} %pad_maximum_fusion.5.rows, ...), custom_call_target="tpu_custom_call" | custom-call | tf_op jit(solution)/shard_map/pallas_call | solution.py:308
  113.9 1.1 pad_maximum_fusion.9.refs_0_
  115.0 1.3 collective-permute-done.8.final_theirs
  116.3 13.3 %shard_map.379 = (f32[256,1024]{1,0:T(8,128)}, bf16[2,2,256,128]{3,2,1,0:T(8,128)(2,1)}, bf16[512,128]{1,0:T(8,128)(2,1)}, bf16[1024,1280]{1,0:T(8,128)(2,1)}, f...) custom-call(s32[3]{0:T(128)} %pad_add_fusion.4.spot, f32[512,1024]{1,0:T(8,128)} %get-tuple-element.82.resid, ...), custom_call_target="tpu_custom_call" | custom-call | tf_op jit(solution)/shard_map/pallas_call | solution.py:419
  129.6 62.9 %shard_map.380 = (bf16[10,256,128]{2,1,0:T(8,128)(2,1)}, bf16[10,256,128]{2,1,0:T(8,128)(2,1)}, f32[2,128]{1,0:T(2,128)}, bf16[2048,128]{1,0:T(8,128)(2,1)}, bf1...) custom-call(bf16[2,2,256,128]{3,2,1,0:T(8,128)(2,1)} %get-tuple-elem, ...), custom_call_target="tpu_custom_call" | custom-call | tf_op jit(solution)/shard_map/pallas_call | solution.py:776
  192.5 1.8 broadcast_select_fusion.1
  194.4 1.0 copy.77
  196.1 28.4 %shard_map.381 = (bf16[1024,1024]{1,0:T(8,128)(2,1)}, bf16[1024,1920]{1,0:T(8,128)(2,1)}) custom-call(s32[3]{0:T(128)} %pad_add_fusion.4.spot, bf16[10,256,128]{2,1,0:T(8,128)(2,1)} %get-tuple-element.98.own, bf16[10,256,128]{2,1,0:T(8,128)(2,1)} %get-tuple-element.99.peer, bf16[1024,1024]{1,0:T(8,128)(2,1)} %get-tuple-element.100.normed, ...), custom_call_target="tpu_custom_call" | custom-call | tf_op jit(solution)/shard_map/pallas_call | solution.py:475
  224.5 58.8 %shard_map.382 = (f32[256,1024]{1,0:T(8,128)}, f32[88,128]{1,0:T(8,128)}, f32[32,1024]{1,0:T(8,128)}, f32[2,8,2048]{2,1,0:T(8,128)}, f32[2,8,1280]{2,1,0:T(8,128...) custom-call(bf16[2,256,1024]{2,1,0:T(8,128)(2,1)} %pad_maximum_fusion.9.refs_0_, bf16[4,256,1024]{2,1,0:T(8,128)(2,1)} %bitcast.78, ...), custom_call_target="tpu_custom_call" | custom-call | tf_op jit(solution)/shard_map/pallas_call | solution.py:949
  286.2 1.8 shard_map.383
  288.0 1.4 fusion.10
  292.7 2.3 copy.84
  295.0 1.6 copy.85
  (99 shorter events, 21.8 us)
Async XLA Ops:
  0.7 19.7 %collective-permute-start = (bf16[256,1024]{1,0:T(8,128)(2,1)}, bf16[256,1024]{1,0:T(8,128)(2,1)S(1)}, u32[]{:S(2)}, u32[]{:S(2)}) collective-permute-start(bf16[256,1024]{1,0:T(8,128)(2,1)} %bitcast.81), channel_id=1, source_target_pairs={{0,1},{1,0},{2,3},{3,2},{4,5},{5,4},{6,7},{7,6},{8,9},{9,8},{10,11... | collective-permute-start | bytes 1572872 | tf_op jit(solution)/shard_map/ppermute | solution.py:1013
  1.4 19.0 %collective-permute-start.1 = (bf16[256,1024]{1,0:T(8,128)(2,1)}, bf16[256,1024]{1,0:T(8,128)(2,1)S(1)}, u32[]{:S(2)}, u32[]{:S(2)}) collective-permute-start(bf16[256,1024]{1,0:T(8,128)(2,1)} %bitcast.79), channel_id=1, source_target_pairs={{0,1},{1,0},{2,3},{3,2},{4,5},{5,4},{6,7},{7,6},{8,9},{9,8},{10,11... | collective-permute-start | bytes 1572872 | tf_op jit(solution)/shard_map/ppermute | solution.py:1013
  3.0 5.4 %copy-start.7 = (s32[256,8]{0,1:T(8,128)}, s32[256,8]{0,1:T(8,128)S(1)}, u32[]{:S(2)}) copy-start(s32[256,8]{0,1:T(8,128)S(1)} %reshape_squeeze.7) | copy-start | bytes 24580
  3.0 15.8 %collective-permute-start.2 = (s32[768,8]{0,1:T(8,128)S(1)}, s32[768,8]{0,1:T(8,128)S(1)}, u32[]{:S(2)}, u32[]{:S(2)}) collective-permute-start(s32[768,8]{0,1:T(8,128)S(1)} %pad_add_fusion.1), channel_id=1, source_target_pairs={{0,1},{1,0},{2,3},{3,2},{4,5},{5,4},{6,7},{7,6},{8,9},{9,8},{10,11... | collective-permute-start | bytes 73736 | tf_op jit(solution)/shard_map/ppermute | solution.py:1013
  11.0 9.3 %copy-start.2 = (bf16[1,256,1024]{2,1,0:T(8,128)(2,1)S(1)}, bf16[1,256,1024]{2,1,0:T(8,128)(2,1)}, u32[]{:S(2)}) copy-start(bf16[1,256,1024]{2,1,0:T(8,128)(2,1)} %param.23) | copy-start | bytes 1572868
  11.0 9.3 %copy-start.3 = (bf16[1,256,1024]{2,1,0:T(8,128)(2,1)S(1)}, bf16[1,256,1024]{2,1,0:T(8,128)(2,1)}, u32[]{:S(2)}) copy-start(bf16[1,256,1024]{2,1,0:T(8,128)(2,1)} %param.24) | copy-start | bytes 1572868
  18.8 0.6 copy-start.10
  35.4 7.0 %copy-start.16 = (bf16[128,1024]{1,0:T(8,128)(2,1)S(1)}, bf16[128,1024]{1,0:T(8,128)(2,1)}, u32[]{:S(2)}) copy-start(bf16[128,1024]{1,0:T(8,128)(2,1)} %get-tuple-element.77) | copy-start | bytes 786436
  37.6 18.1 %collective-permute-start.3 = (bf16[10,256,128]{2,1,0:T(8,128)(2,1)S(1)}, bf16[10,256,128]{2,1,0:T(8,128)(2,1)S(1)}, u32[]{:S(2)}, u32[]{:S(2)}) collective-permute-start(bf16[10,256,128]{2,1,0:T(8,128)(2,1)S(1)} %get-tuple-element.130), channel_id=1, source_target_pairs={{0,2},{2,0},{1,3},{3,1},{4,6},{6,4},{5,7},{7,5},{8,10},{10,8},{9,1... | collective-permute-start | bytes 1966088 | tf_op jit(solution)/shard_map/ppermute | solution.py:1017
  42.3 2.1 copy-start
  42.4 28.1 %copy-start.8 = (s32[256,8]{0,1:T(8,128)S(1)}, s32[256,8]{0,1:T(8,128)}, u32[]{:S(2)}) copy-start(s32[256,8]{0,1:T(8,128)} %copy-done.7) | copy-start | bytes 24580
  42.4 28.1 %slice-start = ((s32[768,8]{0,1:T(8,128)}), s32[256,8]{0,1:T(8,128)S(1)}, s32[]{:S(2)}) async-start(s32[768,8]{0,1:T(8,128)} %copy-done.10), calls=%async_computation | async-start | bytes 16384 | tf_op jit(solution)/shard_map/slice | solution.py:1059
  44.5 37.8 %copy-start.12 = (bf16[1024]{0:T(1024)(128)(2,1)S(1)}, bf16[1024]{0:T(1024)(128)(2,1)}, u32[]{:S(2)}) copy-start(bf16[1024]{0:T(1024)(128)(2,1)} %param.40) | copy-start | bytes 6148
  44.5 38.5 %copy-start.11 = (bf16[4096]{0:T(1024)(128)(2,1)S(1)}, bf16[4096]{0:T(1024)(128)(2,1)}, u32[]{:S(2)}) copy-start(bf16[4096]{0:T(1024)(128)(2,1)} %param.43) | copy-start | bytes 24580
  44.5 39.1 %copy-start.13 = (bf16[1024]{0:T(1024)(128)(2,1)S(1)}, bf16[1024]{0:T(1024)(128)(2,1)}, u32[]{:S(2)}) copy-start(bf16[1024]{0:T(1024)(128)(2,1)} %param.41) | copy-start | bytes 6148
  44.5 39.7 %copy-start.14 = (bf16[1024]{0:T(1024)(128)(2,1)S(1)}, bf16[1024]{0:T(1024)(128)(2,1)}, u32[]{:S(2)}) copy-start(bf16[1024]{0:T(1024)(128)(2,1)} %param.45) | copy-start | bytes 6148
  55.8 0.9 copy-start.5
  67.4 5.7 %collective-permute-start.4 = (bf16[2,256,128]{2,1,0:T(8,128)(2,1)S(1)}, bf16[2,256,128]{2,1,0:T(8,128)(2,1)S(1)}, u32[]{:S(2)}, u32[]{:S(2)}) collective-permute-start(bf16[2,256,128]{2,1,0:T(8,128)(2,1)S(1)} %get-tuple-element.136), channel_id=1, source_target_pairs={{0,2},{2,0},{1,3},{3,1},{4,6},{6,4},{5,7},{7,5},{8,10},{10,8},{9,1... | collective-permute-start | bytes 393224 | tf_op jit(solution)/shard_map/ppermute | solution.py:1017
  73.1 0.7 copy-start.6
  80.4 7.1 %collective-permute-start.5 = (bf16[512,1024]{1,0:T(8,128)(2,1)}, bf16[512,1024]{1,0:T(8,128)(2,1)S(1)}, u32[]{:S(2)}, u32[]{:S(2)}) collective-permute-start(bf16[512,1024]{1,0:T(8,128)(2,1)} %get-tuple-element.81.part_mine), channel_id=1, source_target_pairs={{0,1},{1,0},{2,3},{3,2},{4,5},{5,4},{6,7},{7,6},{8,9},{9,8},{10,11... | collective-permute-start | bytes 3145736 | tf_op jit(solution)/shard_map/ppermute | solution.py:1013
  82.1 3.2 %collective-permute-start.6 = (bf16[256,1024]{1,0:T(8,128)(2,1)}, bf16[256,1024]{1,0:T(8,128)(2,1)S(1)}, u32[]{:S(2)}, u32[]{:S(2)}) collective-permute-start(bf16[256,1024]{1,0:T(8,128)(2,1)} %bitcast.88), channel_id=1, source_target_pairs={{0,1},{1,0},{2,3},{3,2},{4,5},{5,4},{6,7},{7,6},{8,9},{9,8},{10,11... | collective-permute-start | bytes 1572872 | tf_op jit(solution)/shard_map/ppermute | solution.py:1013
  87.5 25.4 %copy-start.9 = (s32[1,256,4,2]{1,3,2,0:T(2,128)S(1)}, s32[1,256,4,2]{1,3,2,0:T(2,128)}, u32[]{:S(2)}) copy-start(s32[1,256,4,2]{1,3,2,0:T(2,128)} %param.28) | copy-start | bytes 24580
  87.5 1.0 copy-start.4
  112.5 3.8 %collective-permute-start.7 = (bf16[512,1024]{1,0:T(8,128)(2,1)}, bf16[512,1024]{1,0:T(8,128)(2,1)}, u32[]{:S(2)}, u32[]{:S(2)}) collective-permute-start(bf16[512,1024]{1,0:T(8,128)(2,1)} %get-tuple-element.83.grad_mine), channel_id=1, source_target_pairs={{0,1},{1,0},{2,3},{3,2},{4,5},{5,4},{6,7},{7,6},{8,9},{9,8},{10,11... | collective-permute-start | bytes 3145736 | tf_op jit(solution)/shard_map/ppermute | solution.py:1013
  113.0 3.3 %collective-permute-start.8 = (bf16[256,1024]{1,0:T(8,128)(2,1)}, bf16[256,1024]{1,0:T(8,128)(2,1)}, u32[]{:S(2)}, u32[]{:S(2)}) collective-permute-start(bf16[256,1024]{1,0:T(8,128)(2,1)} %get-tuple-element.86), channel_id=1, source_target_pairs={{0,1},{1,0},{2,3},{3,2},{4,5},{5,4},{6,7},{7,6},{8,9},{9,8},{10,11... | collective-permute-start | bytes 1572872 | tf_op jit(solution)/shard_map/ppermute | solution.py:1013
  129.6 62.9 %copy-start.1 = (bf16[32,64,512]{2,1,0:T(8,128)(2,1)S(1)}, bf16[32,64,512]{2,1,0:T(8,128)(2,1)}, u32[]{:S(2)}) copy-start(bf16[32,64,512]{2,1,0:T(8,128)(2,1)} %copy-done) | copy-start | bytes 6291460
  192.5 2.9 copy-start.15
